TPU v7x, 512 devices: a whole 4x8x8 slice. The times are simulated.
512 devices in a mesh: ctx: 64 (over y, z_lo, core), head: 8 (over z_hi, x).
Axes of the slice: x: 4, y: 8, z: 8 (z_hi: 2, z_lo: 4; z = z_hi * 4 + z_lo), core: 2. Of those that a mesh axis runs over, the one named last changes fastest.
Arguments:
- hidden_in: bfloat16 [8192, 4096], P('ctx'), may hold values from -3 to 3
- positions: int32 [8192], P('ctx'), may hold values from 0 to 8191, as said below
- w_query: bfloat16 [4096, 4096], P('ctx', 'head'), may hold values from -0.5 to 0.5
- w_key: bfloat16 [4096, 1024], P('ctx', 'head'), may hold values from -0.5 to 0.5
- w_value: bfloat16 [4096, 1024], P('ctx', 'head'), may hold values from -0.5 to 0.5
- w_out: bfloat16 [4096, 4096], P('head', 'ctx'), may hold values from -0.5 to 0.5
- norm_gain: float32 [4096], replicated, may hold values from 0.1 to 1.9
Outputs:
- normed: bfloat16 [8192, 4096], P(('ctx', 'head'))
Inputs may be any that keep to these rules, and one draw needn't show every extreme that they name: Each aligned block of 64 rows holds exactly the positions of that block's range of 64 rows, each once, in some order.
All inputs are finite; a program needn't handle non-finite values.
Results may differ from a plain program's by a relative error of at most 0.02.
Values may be sent and summed in bfloat16 or wider, within the bound.
A program may use at most 64 MiB of HBM per device.

v0:
```python
import jax
import jax.numpy as jnp
from jax import lax
from jax.sharding import PartitionSpec as P

QH = 32
KVH = 8
HD = 128


NEGATIVE = -1e30


def shifted(value, axis, steps):
    count = lax.axis_size(axis)
    pairs = [(source, (source + steps) % count) for source in range(count)]
    return lax.ppermute(value, axis, pairs)


def rotate(values, places):
    half = HD // 2
    inverse = 500000.0 ** (-(jnp.arange(half, dtype=jnp.float32) * 2.0 / HD))
    angle = places.astype(jnp.float32)[:, None, None] * inverse[None, None, :]
    cosine = jnp.cos(angle)
    sine = jnp.sin(angle)
    first = values[..., :half]
    second = values[..., half:]
    return jnp.concatenate(
        [first * cosine - second * sine, second * cosine + first * sine], axis=-1
    )


def on_device(hidden_in, positions, w_query, w_key, w_value, w_out, norm_gain):
    count = lax.axis_size("ctx")
    here = lax.axis_index("ctx")
    tok = hidden_in.shape[0]
    q_cols = w_query.shape[1]
    kv_cols = w_key.shape[1]
    kv_local = kv_cols // HD
    ratio = QH // KVH
    pieces = (
        lax.all_gather(w_query, "ctx", axis=0, tiled=True),
        lax.all_gather(w_key, "ctx", axis=0, tiled=True),
        lax.all_gather(w_value, "ctx", axis=0, tiled=True),
    )
    rows = pieces[0].shape[0]
    part = hidden_in
    q_full, k_full, v_full = tuple(
        (jnp.dot(part, piece, preferred_element_type=jnp.float32) for piece in pieces)
    )
    query = rotate(q_full.reshape(tok, -1, HD), positions).astype(jnp.bfloat16).reshape(tok, q_cols)
    key = rotate(k_full.reshape(tok, -1, HD), positions).astype(jnp.bfloat16).reshape(tok, kv_cols)
    value = v_full.astype(jnp.bfloat16)
    rounds = tok // count
    target = positions % count * rounds + positions // count - here * rounds

    def place(rows):
        return jnp.zeros_like(rows).at[target].set(rows)

    query, key, value = (
        lax.all_to_all(place(query), "ctx", split_axis=0, concat_axis=0, tiled=True),
        lax.all_to_all(place(key), "ctx", split_axis=0, concat_axis=0, tiled=True),
        lax.all_to_all(place(value), "ctx", split_axis=0, concat_axis=0, tiled=True),
    )
    q_places = jnp.arange(tok, dtype=jnp.int32) * count + here
    grouped = (
        query.reshape(tok, kv_local, ratio, HD)
        .transpose(1, 2, 0, 3)
        .reshape(kv_local, ratio * tok, HD)
    )
    row_places = jnp.tile(q_places, ratio)
    latest = jnp.max(q_places)
    scale = 1.0 / jnp.sqrt(jnp.float32(HD))

    def update(state, block):
        k_block, v_block, k_places = block
        peak, total, summed = state

        def compute(unused):
            k_group = k_block.reshape(-1, kv_local, HD)
            v_group = v_block.reshape(-1, kv_local, HD)
            score = (
                jnp.einsum("grd,kgd->grk", grouped, k_group, preferred_element_type=jnp.float32)
                * scale
            )
            visible = k_places[None, None, :] <= row_places[None, :, None]
            score = jnp.where(visible, score, NEGATIVE)
            fresh = jnp.maximum(peak, jnp.max(score, axis=-1))
            fade = jnp.exp(peak - fresh)
            weight = jnp.where(visible, jnp.exp(score - fresh[..., None]), 0.0)
            new_total = total * fade + jnp.sum(weight, axis=-1)
            product = jnp.einsum(
                "grk,kgd->grd",
                weight.astype(jnp.bfloat16),
                v_group,
                preferred_element_type=jnp.float32,
            )
            return (fresh, new_total, summed * fade[..., None] + product)

        def keep(unused):
            return (peak, total, summed)

        return lax.cond(jnp.min(k_places) <= latest, compute, keep, None)

    start_state = (
        jnp.full((kv_local, ratio * tok), NEGATIVE, jnp.float32),
        jnp.zeros((kv_local, ratio * tok), jnp.float32),
        jnp.zeros((kv_local, ratio * tok, HD), jnp.float32),
    )
    own = (key, value, q_places)

    def cycle_step(step, carry):
        block, inner = carry
        block = shifted((block[0], block[1], block[2]), "ctx", 1)
        return (block, update(inner, block))

    unused_block, state = lax.fori_loop(0, count - 1, cycle_step, (own, update(start_state, own)))
    peak, total, summed = state
    attended = (
        (summed / total[..., None])
        .reshape(kv_local, ratio, tok, HD)
        .transpose(2, 0, 1, 3)
        .reshape(tok, q_cols)
        .astype(jnp.bfloat16)
    )
    returned = lax.all_to_all(attended, "ctx", split_axis=0, concat_axis=0, tiled=True)
    attended = returned[target]
    out_weight = lax.all_gather(w_out, "ctx", axis=1, tiled=True)
    heads = lax.axis_size("head")
    share = tok // heads
    part = attended
    mixed = lax.psum_scatter(
        jnp.dot(part, out_weight, preferred_element_type=jnp.float32).astype(jnp.bfloat16),
        "head",
        scatter_dimension=0,
        tiled=True,
    ).astype(jnp.float32)
    own_rows = lax.dynamic_slice_in_dim(hidden_in, lax.axis_index("head") * share, share, 0).astype(
        jnp.float32
    )
    residual = own_rows + mixed
    spread = jnp.mean(residual * residual, axis=-1, keepdims=True)
    return (residual * lax.rsqrt(spread + 1e-05) * norm_gain).astype(jnp.bfloat16)


def solution(mesh):
    return jax.shard_map(
        on_device,
        mesh=mesh,
        in_specs=(
            P("ctx", None),
            P("ctx"),
            P("ctx", "head"),
            P("ctx", "head"),
            P("ctx", "head"),
            P("head", "ctx"),
            P(),
        ),
        out_specs=P(("ctx", "head"), None),
        check_vma=False,
    )
```

profile of v0, /device:TPU:1, one launch (start us, length us, event | category | flops | bytes accessed | tf_op | source)
XLA Modules:
  0.0 1624.2 jit_solution(2485502123745399285)
XLA Ops:
  11.0 121.5 %all-gather.7.cloned.1.call-done = bf16[4096,128]{1,0:T(8,128)(2,1)} async-done(((bf16[64,128]{1,0:T(8,128)(2,1)}), bf16[4096,128]{1,0:T(8,128)(2,1)}) %all-gather.7.cloned.1.call-update) | async-done | bytes 1048592 | tf_op jit(solution)/shard_map/all_gather | solution.py:44
  135.9 7.0 all-to-all-start.1
  142.9 106.3 %all-gather.5.cloned.1.call-done = bf16[4096,128]{1,0:T(8,128)(2,1)} async-done(((bf16[64,128]{1,0:T(8,128)(2,1)}), bf16[4096,128]{1,0:T(8,128)(2,1)}) %all-gather.5.cloned.1.call-update) | async-done | bytes 1048592 | tf_op jit(solution)/shard_map/all_gather | solution.py:43
  251.2 118.2 %all-gather.9.cloned.1.call-done = bf16[4096,512]{1,0:T(8,128)(2,1)} async-done(((bf16[64,512]{1,0:T(8,128)(2,1)}), bf16[4096,512]{1,0:T(8,128)(2,1)}) %all-gather.9.cloned.1.call-update) | async-done | bytes 4194320 | tf_op jit(solution)/shard_map/all_gather | solution.py:42
  374.7 7.1 all-to-all-start.2
  383.6 9.3 all-to-all-done.2
  399.5 7.6 all-to-all-done
  410.3 1089.6 %while.21 = (s32[]{:T(128)}, bf16[128,128]{1,0:T(8,128)(2,1)S(1)}, bf16[128,128]{1,0:T(8,128)(2,1)S(1)}, s32[128]{0:T(128)S(1)}, f32[1,512]{1,0:T(1,128)}, /*ind...) while((s32[]{:T(128)}, bf16[128,128]{1,0:T(8,128)(2,1)S(1)}, ...), condition=%wide.region_15.16_spmd.clone, body=%wide.region_9.15_spmd.clone.sunk | while | flops 34473088 | bytes 1947515 | solution.py:117
  498.2 6.8 collective-permute-done.2
  515.6 6.8 collective-permute-done.2
  550.3 6.8 collective-permute-done.2
  567.7 6.8 collective-permute-done.2
  585.1 6.8 collective-permute-done.2
  619.8 6.8 collective-permute-done.2
  637.2 6.8 collective-permute-done.2
  706.7 6.8 collective-permute-done.2
  758.8 6.8 collective-permute-done.2
  828.3 6.8 collective-permute-done.2
  880.4 6.8 collective-permute-done.2
  949.8 6.8 collective-permute-done.2
  1002.0 6.8 collective-permute-done.2
  1071.4 6.8 collective-permute-done.2
  1123.6 6.8 collective-permute-done.2
  1193.0 6.8 collective-permute-done.2
  1245.1 6.8 collective-permute-done.2
  1314.6 6.8 collective-permute-done.2
  1366.7 6.8 collective-permute-done.2
  1436.2 6.8 collective-permute-done.2
  1488.3 6.8 collective-permute-done.2
  1500.9 10.4 all-to-all-start.3
  1511.4 11.0 all-to-all-done.3
  1528.0 87.0 %reduce-scatter.2.cloned.1.call-done = bf16[16,4096]{1,0:T(8,128)(2,1)} async-done(((bf16[128,4096]{1,0:T(8,128)(2,1)}), bf16[16,4096]{1,0:T(8,128)(2,1)}) %reduce-scatter.2.cloned.1.call-update) | async-done | bytes 131088 | tf_op jit(solution)/shard_map/reduce_scatter | solution.py:132
  (1168 shorter events, 1058.7 us)
Async XLA Ops:
  6.5 125.9 %all-gather.7.cloned.1.call-start = ((), (), s32[]{:S(2)}) async-start(), calls=%async_computation.6 | async-start | bytes 1064960 | tf_op jit(solution)/shard_map/all_gather | solution.py:44
  7.3 241.9 %all-gather.5.cloned.1.call-start = ((), (), s32[]{:S(2)}) async-start(), calls=%async_computation.5 | async-start | bytes 1064960 | tf_op jit(solution)/shard_map/all_gather | solution.py:43
  8.0 361.4 %all-gather.9.cloned.1.call-start = ((), (), s32[]{:S(2)}) async-start(), calls=%async_computation.7 | async-start | bytes 4259840 | tf_op jit(solution)/shard_map/all_gather | solution.py:42
  8.7 1514.6 %all-gather.11.cloned.1.call-start = ((), (), s32[]{:S(2)}) async-start(), calls=%async_computation.8 | async-start | bytes 4259840 | tf_op jit(solution)/shard_map/all_gather | solution.py:128
  135.9 238.8 %all-to-all-start.1 = ((bf16[64,2,128]{2,1,0:T(2,128)(2,1)}), bf16[64,2,128]{2,1,0:T(2,128)(2,1)S(1)}, u32[]{:S(2)}, u32[]{:S(2)}) async-start(bf16[64,2,128]{2,1,0:T(2,128)(2,1)} %bitcast.17), calls=%async_computation.1 | async-start | bytes 65536 | tf_op jit(solution)/shard_map/all_to_all | solution.py:63
  374.7 18.2 %all-to-all-start.2 = ((bf16[64,2,512]{2,1,0:T(2,128)(2,1)}), bf16[64,2,512]{2,1,0:T(2,128)(2,1)S(1)}, u32[]{:S(2)}, u32[]{:S(2)}) async-start(bf16[64,2,512]{2,1,0:T(2,128)(2,1)} %all_to_all.34), calls=%async_computation.2 | async-start | bytes 262144 | tf_op jit(solution)/shard_map/all_to_all | solution.py:61
  440.3 14.7 collective-permute-start.1
  457.7 14.7 collective-permute-start.1
  492.4 14.7 collective-permute-start.1
  509.8 14.7 collective-permute-start.1
  544.6 14.7 collective-permute-start.1
  561.9 14.7 collective-permute-start.1
  579.3 14.7 collective-permute-start.1
  614.0 14.7 collective-permute-start.1
  631.4 14.7 collective-permute-start.1
  700.9 14.7 collective-permute-start.1
  753.0 14.7 collective-permute-start.1
  822.5 14.7 collective-permute-start.1
  874.6 14.7 collective-permute-start.1
  944.1 14.7 collective-permute-start.1
  996.2 14.7 collective-permute-start.1
  1048.3 14.7 collective-permute-start.1
  1065.7 14.7 collective-permute-start.1
  1117.8 14.7 collective-permute-start.1
  1187.2 14.7 collective-permute-start.1
  1239.4 14.7 collective-permute-start.1
  1308.8 14.7 collective-permute-start.1
  1361.0 14.7 collective-permute-start.1
  1430.4 14.7 collective-permute-start.1
  1482.5 14.7 collective-permute-start.1
  1500.9 21.5 %all-to-all-start.3 = ((bf16[64,2,512]{2,1,0:T(2,128)(2,1)}), bf16[64,2,512]{2,1,0:T(2,128)(2,1)S(1)}, u32[]{:S(2)}, u32[]{:S(2)}) async-start(bf16[64,2,512]{2,1,0:T(2,128)(2,1)} %convert_element_type.63), calls=%async_computation.3 | async-start | bytes 262144 | tf_op jit(solution)/shard_map/all_to_all | solution.py:126
  1511.3 103.6 %reduce-scatter.2.cloned.1.call-start = ((), (), s32[]{:S(2)}) async-start(), calls=%async_computation.9 | async-start | bytes 1179648 | tf_op jit(solution)/shard_map/reduce_scatter | solution.py:132
  (168 other events, 2402.3 us)
Sparse Core Ops, SparseCore 0:
  9.5 122.9 all-gather.6
  134.6 114.5 all-gather.4
  251.3 118.0 all-gather.8
  371.4 118.4 all-gather.10
  1528.1 86.7 reduce-scatter.1
where the time goes:
time: 1640 us; the launch traced here: 1620 us
  waiting for transfers between devices  880 us (54%)
  starting transfers between devices  402 us (25%)
  other arithmetic  146 us (9%)
  loops' own time  91.9 us (6%)
  matrix products  45.8 us (3%)
  local copies, waits for them, and re-layouts  44 us (3%)
    ppermute x189, waiting for transfers between devices, shifted(): return lax.ppermute(value, axis, pairs)  417 us
    ppermute x189, starting transfers between devices, shifted(): return lax.ppermute(value, axis, pairs)  372 us
    all_gather x1, waiting for transfers between devices, on_device(): lax.all_gather(w_value, 'ctx', axis=0, tiled=True)  121 us
    all_gather x1, waiting for transfers between devices, on_device(): lax.all_gather(w_query, 'ctx', axis=0, tiled=True)  118 us
    all_gather x1, waiting for transfers between devices, on_device(): lax.all_gather(w_key, 'ctx', axis=0, tiled=True)  106 us
    another operation x1, loops' own time, on_device(): lax.fori_loop(0, count - 1, cycle_step, (own, update(start_state, own)))  89.4 us
    reduce_scatter x1, waiting for transfers between devices, on_device(): lax.psum_scatter(jnp.dot(part, out_weight, preferred_element_type=jnp.flo...  87 us
    add x64, other arithmetic, compute(): new_total = total * fade + jnp.sum(weight, axis=-1)  44.7 us
  transfers between devices with their start and end apart: 198, of which 70 were waited for; matrix products, arithmetic and copies ran while one was open for 14% of the time, Pallas kernels for 0%

commit v1 on v0

v1 whole, which is shorter than its diff:
```python
import jax
import jax.numpy as jnp
from jax import lax
from jax.sharding import PartitionSpec as P

QH = 32
KVH = 8
HD = 128
NEGATIVE = -1e30


def rotate(values, places):
    half = HD // 2
    inverse = 500000.0 ** (-(jnp.arange(half, dtype=jnp.float32) * 2.0 / HD))
    angle = places.astype(jnp.float32)[:, None, None] * inverse[None, None, :]
    cosine = jnp.cos(angle)
    sine = jnp.sin(angle)
    first = values[..., :half]
    second = values[..., half:]
    return jnp.concatenate(
        [first * cosine - second * sine, second * cosine + first * sine], axis=-1
    )


def on_device(hidden_in, positions, w_query, w_key, w_value, w_out, norm_gain):
    here = lax.axis_index("ctx")
    tok = hidden_in.shape[0]
    q_cols = w_query.shape[1]
    kv_cols = w_key.shape[1]
    ratio = QH // KVH
    joined = jnp.concatenate([w_query, w_key, w_value], axis=1)
    w_all = lax.all_gather(joined, "ctx", axis=0, tiled=True)
    out_weight = lax.all_gather(w_out.T, "ctx", axis=0, tiled=True)
    full = jnp.dot(hidden_in, w_all, preferred_element_type=jnp.float32)
    turned = rotate(
        full[:, : q_cols + kv_cols].reshape(tok, -1, HD), positions
    ).astype(jnp.bfloat16)
    value = full[:, q_cols + kv_cols :].astype(jnp.bfloat16)
    key = turned[:, ratio:].reshape(tok, kv_cols)
    kv = lax.all_gather(
        jnp.concatenate([key, value], axis=1), "ctx", axis=0, tiled=True
    )
    keys, values = kv[:, :HD], kv[:, HD:]
    rows = turned[:, :ratio].transpose(1, 0, 2).reshape(ratio * tok, HD)
    score = jnp.einsum(
        "rd,kd->rk", rows, keys, preferred_element_type=jnp.float32
    ) * (1.0 / jnp.sqrt(jnp.float32(HD)))
    column = jnp.arange(keys.shape[0], dtype=jnp.int32)
    spread_places = jnp.where(
        column < here * tok, -1, jnp.where(column >= (here + 1) * tok, 1 << 30, 0)
    )
    spread_places = lax.dynamic_update_slice(spread_places, positions, (here * tok,))
    row_places = jnp.tile(positions, ratio)
    visible = spread_places[None, :] <= row_places[:, None]
    score = jnp.where(visible, score, NEGATIVE)
    peak = jnp.max(score, axis=-1, keepdims=True)
    weight = jnp.exp(score - peak)
    total = jnp.sum(weight, axis=-1, keepdims=True)
    summed = jnp.dot(
        weight.astype(jnp.bfloat16), values, preferred_element_type=jnp.float32
    )
    attended = (
        (summed / total)
        .reshape(ratio, tok, HD)
        .transpose(1, 0, 2)
        .reshape(tok, q_cols)
        .astype(jnp.bfloat16)
    )
    heads = lax.axis_size("head")
    share = tok // heads
    product = lax.dot_general(
        attended, out_weight, (((1,), (1,)), ((), ())), preferred_element_type=jnp.float32
    ).astype(jnp.bfloat16)
    mixed = lax.psum_scatter(product, "head", scatter_dimension=0, tiled=True).astype(
        jnp.float32
    )
    own_rows = lax.dynamic_slice_in_dim(
        hidden_in, lax.axis_index("head") * share, share, 0
    ).astype(jnp.float32)
    residual = own_rows + mixed
    spread = jnp.mean(residual * residual, axis=-1, keepdims=True)
    return (residual * lax.rsqrt(spread + 1e-05) * norm_gain).astype(jnp.bfloat16)


def solution(mesh):
    return jax.shard_map(
        on_device,
        mesh=mesh,
        in_specs=(
            P("ctx", None),
            P("ctx"),
            P("ctx", "head"),
            P("ctx", "head"),
            P("ctx", "head"),
            P("head", "ctx"),
            P(),
        ),
        out_specs=P(("ctx", "head"), None),
        check_vma=False,
    )
```

time: 1640 us -> 490 us (0.30)
  waiting for transfers between devices: 880 us -> 434 us
  starting transfers between devices: 402 us -> 0.12 us
  other arithmetic: 146 us -> 14.3 us
  loops' own time: 91.9 us -> 0 us
  local copies, waits for them, and re-layouts: 44 us -> 0.59 us
  matrix products: 45.8 us -> 26.8 us
    ppermute x189 -> x0, waiting for transfers between devices: 417 us -> none  [shifted(): return lax.ppermute(value, axis, pairs)]
    ppermute x189 -> x0, starting transfers between devices: 372 us -> none  [shifted(): return lax.ppermute(value, axis, pairs)]
    another operation x65 -> x0, loops' own time: 91.9 us -> none  [the longest x1 89.4 us: on_device(): lax.fori_loop(0, count - 1, cycle_step, (own, update(start_state, own)))]
    add x65 -> x0, other arithmetic: 45.4 us -> none  [the longest x64 44.7 us: compute(): new_total = total * fade + jnp.sum(weight, axis=-1)]
    reduce_min x64 -> x0, other arithmetic: 44.4 us -> none  [update(): return lax.cond(jnp.min(k_places) <= latest, compute, keep, None)]
    max x63 -> x0, other arithmetic: 43.4 us -> none  [compute(): fresh = jnp.maximum(peak, jnp.max(score, axis=-1))]
    cond x63 -> x0, local copies, waits for them, and re-layouts: 36.6 us -> none
    all_to_all x4 -> x0, starting transfers between devices: 29.1 us -> none  [the longest x1 10.4 us: on_device(): lax.all_to_all(attended, 'ctx', split_axis=0, concat_axis=0, tiled=True)]
  transfers between devices with their start and end apart: 198 -> 4, of which waited for: 70 -> 4; matrix products, arithmetic and copies ran while one was open for 14% -> 6% of each run, Pallas kernels for 0% -> 0%
where the time goes in v1:
time: 490 us; the launch traced here: 489 us
  waiting for transfers between devices  434 us (89%)
  matrix products  26.8 us (5%)
  other arithmetic  14.3 us (3%)
  between operations  13.2 us (3%)
    all_gather x1, waiting for transfers between devices, on_device(): w_all = lax.all_gather(joined, 'ctx', axis=0, tiled=True)  130 us
    all_gather x1, waiting for transfers between devices, on_device(): lax.all_gather(jnp.concatenate([key, value], axis=1), 'ctx', axis=0, tile...  120 us
    all_gather x1, waiting for transfers between devices, on_device(): out_weight = lax.all_gather(w_out.T, 'ctx', axis=0, tiled=True)  93.8 us
    reduce_scatter x1, waiting for transfers between devices, on_device(): lax.psum_scatter(product, 'head', scatter_dimension=0, tiled=True)  88.9 us
  transfers between devices with their start and end apart: 4, of which 4 were waited for; matrix products, arithmetic and copies ran while one was open for 6% of the time, Pallas kernels for 0%

profile of v1, /device:TPU:1, one launch (start us, length us, event | category | flops | bytes accessed | tf_op | source)
XLA Modules:
  0.0 488.6 jit_solution(15626103396227609372)
XLA Ops:
  6.5 0.0 copy-start.2
  6.5 0.0 all-gather.4.cloned.1.call-start
  6.5 1.5 pad_maximum_fusion
  8.1 0.0 all-gather.4.cloned.1.call-update
  8.1 0.0 all-gather.6.cloned.1.call-start
  8.1 0.7 convert_element_type.33
  8.8 0.2 multiply_cosine_fusion
  9.0 129.7 %all-gather.4.cloned.1.call-done = bf16[4096,768]{1,0:T(8,128)(2,1)} async-done(((bf16[64,768]{1,0:T(8,128)(2,1)}), bf16[4096,768]{1,0:T(8,128)(2,1)}) %all-gather.4.cloned.1.call-update) | async-done | bytes 6291472 | tf_op jit(solution)/shard_map/all_gather | solution.py:32
  138.7 4.9 convolution_bitcast_fusion
  143.6 0.1 subtract_convert_fusion
  143.7 0.6 pad_maximum_fusion.1
  144.4 0.0 all-gather.6.cloned.1.call-update
  144.4 0.0 all-gather.8.cloned.1.call-start
  144.4 0.7 all-gather.8.cloned.1.call-update
  145.1 0.0 reduce-scatter.2.cloned.1.call-start
  145.2 0.0 copy-done.2
  145.2 0.3 dynamic_update_slice.5
  145.5 0.1 copy.8
  145.6 120.4 %all-gather.6.cloned.1.call-done = bf16[8192,256]{0,1:T(8,128)(2,1)} async-done(((bf16[128,256]{0,1:T(8,128)(2,1)}), bf16[8192,256]{0,1:T(8,128)(2,1)}) %all-gather.6.cloned.1.call-update) | async-done | bytes 4194320 | tf_op jit(solution)/shard_map/all_gather | solution.py:40
  266.0 8.9 %fusion.20 = (f32[512]{0:T(512)S(1)}, f32[512,8192]{1,0:T(8,128)}) fusion(bf16[512,128]{1,0:T(8,128)(2,1)S(1)} %bitcast.23, bf16[8192,256]{0,1:T(8,128)(2,1)} %all-gather.6.cloned.1.call-done, s32[512]{0:T(512)S(1)} %broadcast_bitcast_fusion, s32[8192]{0:T(1024)S(1)} %dynamic_update_slice.5), kind=kOutput, calls=%fused_computation.34 | convolution fusion | flops 1090518528 | bytes 19042304 | tf_op jit(solution)/shard_map/rd,kd->rk/dot_general | solution.py:45
  275.0 8.3 %fusion = f32[512]{0:T(512)S(1)} fusion(f32[512,8192]{1,0:T(8,128)} %get-tuple-element.10, f32[512]{0:T(512)S(1)} %get-tuple-element.9), kind=kLoop, calls=%fused_computation.2 | loop fusion | flops 8388096 | bytes 16781312 | tf_op jit(solution)/shard_map/reduce_sum | solution.py:58
  283.3 0.0 copy-done
  283.3 0.0 copy-start.1
  283.3 8.4 %fusion.12 = bf16[512,128]{1,0:T(8,128)(2,1)S(1)} fusion(bf16[8192,256]{0,1:T(8,128)(2,1)S(1)} %copy-done, f32[512,8192]{1,0:T(8,128)} %get-tuple-element.10, f32[512]{0:T(512)S(1)} %get-tuple-element.9, f32[512]{0:T(512)S(1)} %fusion), kind=kOutput, calls=%fused_computation.11 | convolution fusion | flops 1082261504 | bytes 19009536 | tf_op jit(solution)/shard_map/dot_general | solution.py:59
  291.7 0.1 copy.9
  291.8 93.8 %all-gather.8.cloned.1.call-done = bf16[4096,512]{1,0:T(8,128)(2,1)} async-done(((bf16[64,512]{1,0:T(8,128)(2,1)}), bf16[4096,512]{1,0:T(8,128)(2,1)}) %all-gather.8.cloned.1.call-update) | async-done | bytes 4194320 | tf_op jit(solution)/shard_map/all_gather | solution.py:33
  385.6 4.6 convolution_convert_fusion
  390.3 0.0 reduce-scatter.2.cloned.1.call-update
  390.3 88.9 %reduce-scatter.2.cloned.1.call-done = bf16[16,4096]{1,0:T(8,128)(2,1)} async-done(((bf16[128,4096]{1,0:T(8,128)(2,1)}), bf16[16,4096]{1,0:T(8,128)(2,1)}) %reduce-scatter.2.cloned.1.call-update) | async-done | bytes 131088 | tf_op jit(solution)/shard_map/reduce_scatter | solution.py:74
  479.2 1.1 multiply_reduce_fusion
  480.4 0.0 copy-done.1
  480.4 1.7 multiply_convert_fusion
  (9 shorter events, 0.1 us)
Async XLA Ops:
  6.5 138.7 %copy-start.2 = (s32[128]{0:T(128)S(1)}, s32[128]{0:T(128)}, u32[]{:S(2)}) copy-start(s32[128]{0:T(128)} %param.8) | copy-start | bytes 1540
  6.5 132.2 %all-gather.4.cloned.1.call-start = ((), (), s32[]{:S(2)}) async-start(), calls=%async_computation.1 | async-start | bytes 6389760 | tf_op jit(solution)/shard_map/all_gather | solution.py:32
  8.1 257.9 %all-gather.6.cloned.1.call-start = ((), (), s32[]{:S(2)}) async-start(), calls=%async_computation.2 | async-start | bytes 4259840 | tf_op jit(solution)/shard_map/all_gather | solution.py:40
  144.4 241.3 %all-gather.8.cloned.1.call-start = ((), (), s32[]{:S(2)}) async-start(), calls=%async_computation.3 | async-start | bytes 4259840 | tf_op jit(solution)/shard_map/all_gather | solution.py:33
  145.1 334.1 %reduce-scatter.2.cloned.1.call-start = ((), (), s32[]{:S(2)}) async-start(), calls=%async_computation.4 | async-start | bytes 1179648 | tf_op jit(solution)/shard_map/reduce_scatter | solution.py:74
  275.0 8.3 %copy-start = (bf16[8192,256]{0,1:T(8,128)(2,1)S(1)}, bf16[8192,256]{0,1:T(8,128)(2,1)}, u32[]{:S(2)}) copy-start(bf16[8192,256]{0,1:T(8,128)(2,1)} %all-gather.6.cloned.1.call-done) | copy-start | bytes 12582916
  283.3 197.1 %copy-start.1 = (f32[4096]{0:T(1024)S(1)}, f32[4096]{0:T(1024)}, u32[]{:S(2)}) copy-start(f32[4096]{0:T(1024)} %param.13) | copy-start | bytes 49156
Sparse Core Ops, SparseCore 0:
  9.5 129.1 all-gather.3
  144.5 121.4 all-gather.5
  268.2 117.3 all-gather.7
  390.4 88.7 reduce-scatter.1

commit v2 on v1

v2 whole, which is shorter than its diff:
```python
import jax
import jax.numpy as jnp
from jax import lax
from jax.experimental import pallas as pl
from jax.experimental.pallas import tpu as pltpu
from jax.sharding import PartitionSpec as P

MESH = pl.DeviceIdType.MESH
HD = 128
ROWS = 8
LINE = 4
CHIPS = ROWS * LINE
WAVES = ROWS // 2 + LINE
O_AT = 5
NEGATIVE = -1e30
SCALE = 1.4426950408889634 / HD ** 0.5
ORDER = (3, 2, 1, 0)


class Place:
    def __init__(self):
        ctx = lax.axis_index("ctx")
        head = lax.axis_index("head")
        self.core = ctx % 2
        self.z = (ctx // 2) % LINE
        self.y = ctx // (2 * LINE)
        self.x = head % 4
        self.zh = head // 4
        self.chip = ctx // 2
        self.ctx = ctx
        self.head = head

    def at(self, y, z, core):
        return ((y * LINE + z) * 2 + core, self.head)

    def sibling(self):
        return (self.chip * 2 + 1 - self.core, self.head)

    def up(self):
        return self.at((self.y + 1) % ROWS, self.z, self.core)

    def down(self):
        return self.at((self.y + ROWS - 1) % ROWS, self.z, self.core)

    def right(self):
        return self.at(self.y, jnp.minimum(self.z + 1, LINE - 1), self.core)

    def left(self):
        return self.at(self.y, jnp.maximum(self.z - 1, 0), self.core)

    def across(self, steps):
        return (self.ctx, self.zh * 4 + (self.x + 4 + steps) % 4)

    def far(self):
        return (self.ctx, (1 - self.zh) * 4 + self.x)

    def order(self, i):
        z = self.z
        if i == 0:
            return z
        a = (1, 0, 3, 2)
        b = (2, 2, 1, 1)
        c = (3, 3, 0, 0)
        t = (a, b, c)[i - 1]
        return jnp.where(z == 0, t[0], jnp.where(z == 1, t[1], jnp.where(z == 2, t[2], t[3])))


class Gather:
    def __init__(self, place, first, last, sems, relay=None):
        self.p = place
        self.first, self.last = first, last
        self.relay = relay
        self.recv, self.by, self.bz, self.ay, self.az = sems

    @staticmethod
    def scratch():
        dma = pltpu.SemaphoreType.DMA
        return [dma((2, CHIPS)), dma((2, CHIPS)), dma((2, LINE)), dma((2, ROWS)), dma((2, CHIPS))]

    def row(self, g):
        d = (g + 1) // 2
        core = self.p.core
        up = jnp.logical_and(g % 2 == 1, jnp.logical_or(g < 7, core == 0))
        return jnp.where(up, self.p.y + ROWS - d, self.p.y + d) % ROWS

    def sends(self, g, i, slot, zq):
        p = self.p
        core = p.core
        up = (g == 0) | (g == 1) | (g == 3) | ((g == 5) & (core == 0))
        down = (g == 0) | (g == 2) | (g == 4) | ((g == 6) & (core == 1))
        if i == 0:
            right, left = p.z < LINE - 1, p.z > 0
        else:
            right = (zq < p.z) & (p.z < LINE - 1)
            left = (zq > p.z) & (p.z > 0)
        s = g * LINE + i

        def copy(part, sem, device):
            ref = (self.first, self.last)[part].at[slot]
            return pltpu.make_async_remote_copy(
                src_ref=ref, dst_ref=ref, send_sem=sem, recv_sem=self.recv.at[part, slot],
                device_id=device, device_id_type=MESH)

        out = []
        out.append((up, lambda: copy(0, self.by.at[0, s], p.up())))
        out.append((down, lambda: copy(0, self.by.at[1, s], p.down())))
        out.append(((g == 0) & right, lambda: copy(0, self.bz.at[0, i], p.right())))
        out.append(((g == 0) & left, lambda: copy(0, self.bz.at[1, i], p.left())))
        if i == 0:
            out.append((up, lambda: copy(1, self.ay.at[0, g], p.up())))
            out.append((down, lambda: copy(1, self.ay.at[1, g], p.down())))
        out.append((right, lambda: copy(1, self.az.at[0, s], p.right())))
        out.append((left, lambda: copy(1, self.az.at[1, s], p.left())))
        return out

    def arrive(self, part, slot):
        ref = (self.first, self.last)[part].at[slot]
        pltpu.make_async_remote_copy(
            src_ref=ref, dst_ref=ref, send_sem=self.recv.at[part, slot],
            recv_sem=self.recv.at[part, slot], device_id=self.p.up(), device_id_type=MESH).wait_recv()

    def step(self, g, i):
        zq = self.p.order(i)
        slot = self.row(g) * LINE + zq

        def wait(part):
            if i == 0:
                pl.when(g > 0)(lambda: self.arrive(part, slot))
            else:
                self.arrive(part, slot)

        out = self.sends(g, i, slot, zq)
        wait(0)
        for cond, make in out[:4]:
            pl.when(cond)(lambda make=make: make().start())
        if self.relay is not None:
            self.relay(0, slot).start()
        wait(1)
        for cond, make in out[4:]:
            pl.when(cond)(lambda make=make: make().start())
        if self.relay is not None:
            self.relay(1, slot).start()

    def wave(self, t):
        for i in ORDER:
            d = t - i
            pl.when((d >= 1) & (d <= 4))(lambda d=d, i=i: self.step(2 * d - 1, i))
            pl.when((d >= 0) & (d <= 3))(lambda d=d, i=i: self.step(2 * d, i))

    def drain(self):
        def one(g, _):
            for i in range(LINE):
                zq = self.p.order(i)
                slot = self.row(g) * LINE + zq
                for cond, make in self.sends(g, i, slot, zq):
                    pl.when(cond)(lambda make=make: make().wait_send())
            return 0
        lax.fori_loop(0, ROWS, one, 0)


def entry(p, extra=()):
    bar = pltpu.get_barrier_semaphore()
    always = [p.sibling(), p.up(), p.down()] + list(extra)
    for d in always:
        pl.semaphore_signal(bar, inc=1, device_id=d, device_id_type=MESH)

    @pl.when(p.z < LINE - 1)
    def _():
        pl.semaphore_signal(bar, inc=1, device_id=p.right(), device_id_type=MESH)

    @pl.when(p.z > 0)
    def _():
        pl.semaphore_signal(bar, inc=1, device_id=p.left(), device_id_type=MESH)

    ends = (p.z == 0).astype(jnp.int32) + (p.z == LINE - 1).astype(jnp.int32)
    pl.semaphore_wait(bar, len(always) + 2 - ends)


def remote(src, dst, send, recv, device):
    return pltpu.make_async_remote_copy(
        src_ref=src, dst_ref=dst, send_sem=send, recv_sem=recv, device_id=device, device_id_type=MESH)


def load_inputs(p, x_ref, wq_ref, wk_ref, wv_ref, aux_ref, hid, aux, wf, wl, loc, snd, rcv):
    core, chip = p.core, p.chip
    tok = x_ref.shape[0]
    depth = wq_ref.shape[0]
    half = wq_ref.shape[1] // 2
    other = 1 - core
    mine = pl.ds(pl.multiple_of(core * half, half), half)
    theirs = pl.ds(pl.multiple_of(other * half, half), half)
    span = pl.ds(pl.multiple_of(core * depth, depth), depth)
    rows = pl.ds(pl.multiple_of(core * tok, tok), tok)
    sib = p.sibling()
    slot_f = wf.at[chip, span]
    slot_l = wl.at[chip, span]
    rem = [
        remote(wq_ref.at[:, theirs], slot_f, snd.at[0], rcv.at[0], sib),
        None,
        remote(x_ref, hid.at[rows], snd.at[2], rcv.at[2], sib),
        remote(aux_ref, aux.at[rows], snd.at[3], rcv.at[3], sib),
    ]
    own = [
        pltpu.make_async_copy(wq_ref.at[:, mine], slot_f, loc.at[0]),
        None,
        pltpu.make_async_copy(x_ref, hid.at[rows], loc.at[2]),
        pltpu.make_async_copy(aux_ref, aux.at[rows], loc.at[3]),
    ]

    @pl.when(core == 0)
    def _():
        remote(wv_ref, slot_l, snd.at[1], rcv.at[1], sib).start()
        pltpu.make_async_copy(wk_ref, slot_l, loc.at[1]).start()

    @pl.when(core == 1)
    def _():
        remote(wk_ref, slot_l, snd.at[1], rcv.at[1], sib).start()
        pltpu.make_async_copy(wv_ref, slot_l, loc.at[1]).start()

    rem[1] = remote(wk_ref, slot_l, snd.at[1], rcv.at[1], sib)
    own[1] = pltpu.make_async_copy(wk_ref, slot_l, loc.at[1])
    for k in (0, 2, 3):
        rem[k].start()
        own[k].start()
    return rem, own


def wait_inputs(rem, own, ks):
    for k in ks:
        own[k].wait()
        rem[k].wait_send()
        rem[k].wait_recv()


def turn(u, cosine, sine):
    return u * cosine + pltpu.roll(u, 64, 1) * sine


def angles(positions):
    half = HD // 2
    inverse = 500000.0 ** (-(jnp.arange(half, dtype=jnp.float32) * 2.0 / HD))
    angle = positions.astype(jnp.float32)[:, None] * inverse[None, :]
    cosine, sine = jnp.cos(angle), jnp.sin(angle)
    return jnp.concatenate([cosine, cosine, -sine, sine], axis=1)

def attend(q_ref, m_ref, l_ref, acc_ref, keys, values, visible=None):
    rows = q_ref.shape[0] // 2
    for h in range(2):
        at = pl.ds(h * rows, rows)
        score = lax.dot_general(q_ref[at], keys, (((1,), (1,)), ((), ())), preferred_element_type=jnp.float32)
        if visible is not None:
            score = jnp.where(visible, score, NEGATIVE)
        before = m_ref[at]
        peak = jnp.maximum(before, jnp.max(score, axis=1, keepdims=True))
        fade = jnp.exp2((before - peak) * SCALE)
        weight = jnp.exp2((score - peak) * SCALE)
        m_ref[at] = peak
        l_ref[at] = l_ref[at] * fade + jnp.sum(weight, axis=1, keepdims=True)
        acc_ref[at] = acc_ref[at] * fade + jnp.dot(
            weight.astype(jnp.bfloat16), values, preferred_element_type=jnp.float32)


def block_kernel(x_ref, wq_ref, wk_ref, wv_ref, wo_ref, aux_ref, gain_ref, out_ref,
                 hid, aux, wf, wl, acc_f, acc_l, kvf, kvl, of, ol, qs, m_ref, l_ref, acc, att,
                 part, xin, zout, zin, fin, tin, loc, snd, rcv, sib_s, sib_r, att_sem, x_s, x_r, z_s, z_r, t_s, t_r, *gsems):
    p = Place()
    core, chip = p.core, p.chip
    tok = x_ref.shape[0]
    sib = p.sibling()
    entry(p, (p.across(1), p.across(-1), p.across(2), p.far()))
    rem, own = load_inputs(p, x_ref, wq_ref, wk_ref, wv_ref, aux_ref, hid, aux, wf, wl, loc, snd, rcv)
    wide = of.shape[2]
    o_own = [pltpu.make_async_copy(wo_ref.at[:, pl.ds(0, wide)], of.at[chip], loc.at[4]),
             pltpu.make_async_copy(wo_ref.at[:, pl.ds(wide, ol.shape[2])], ol.at[chip], loc.at[5])]
    for c in o_own:
        c.start()
    n = len(gsems) // 3
    g_w = Gather(p, wf, wl, gsems[:n])
    g_o = Gather(p, of, ol, gsems[n:2 * n])

    def relay(part_at, slot):
        ref = (kvf, kvl)[part_at].at[core, slot]
        return remote(ref, ref, sib_s.at[part_at, slot], sib_r.at[part_at, slot], sib)

    g_kv = Gather(p, kvf.at[core], kvl.at[core], gsems[2 * n:], relay)
    wait_inputs(rem, own, (0, 1))
    acc_f[...] = jnp.zeros_like(acc_f)
    acc_l[...] = jnp.zeros_like(acc_l)

    def project(t, _):
        g_w.wave(t)

        @pl.when(t == O_AT)
        def _():
            for c in o_own:
                c.wait()
        g_o.wave(t - O_AT)
        d = t - (LINE - 1)

        def use(g):
            row = g_w.row(g)
            depth = LINE * 128
            left = hid[:, pl.ds(pl.multiple_of(row * depth, depth), depth)]
            at = pl.ds(pl.multiple_of(row * LINE, LINE), LINE)
            acc_f[...] += jnp.dot(left, wf[at].reshape(depth, wf.shape[2]), preferred_element_type=jnp.float32)
            acc_l[...] += jnp.dot(left, wl[at].reshape(depth, wl.shape[2]), preferred_element_type=jnp.float32)

        @pl.when(d == 0)
        def _():
            wait_inputs(rem, own, (2, 3))

        pl.when(d >= 1)(lambda: use(2 * d - 1))
        pl.when((d >= 0) & (d <= 3))(lambda: use(2 * d))
        return 0

    lax.fori_loop(0, WAVES, project, 0)

    cosine, sine = aux[:, 0:HD], aux[:, HD:2 * HD]
    last = acc_l[...]
    own_kv = jnp.where(core == 0, turn(last, cosine, sine), last).astype(jnp.bfloat16)
    cut = kvf.shape[2]
    kvf[core, chip] = own_kv[:cut]
    kvl[core, chip] = own_kv[cut:]
    for h in range(2):
        qs[pl.ds(2 * tok * h, 2 * tok)] = turn(acc_f[:, h * HD:(h + 1) * HD], cosine, sine).astype(jnp.bfloat16)
    m_ref[...] = jnp.full_like(m_ref, NEGATIVE)
    l_ref[...] = jnp.zeros_like(l_ref)
    acc[...] = jnp.zeros_like(acc)

    def arrived(slot):
        for part_at in range(2):
            ref = (kvf, kvl)[part_at].at[1 - core, slot]
            remote(ref, ref, sib_s.at[part_at, slot], sib_r.at[part_at, slot], sib).wait_recv()

    def block(kind, start, count):
        at = pl.ds(start, count)
        return jnp.concatenate([kvf[kind, at].reshape(count * cut, HD),
                                kvl[kind, at].reshape(count * (2 * tok - cut), HD)], axis=0)

    def look(t, _):
        g_kv.wave(t)
        g_o.wave(t + WAVES - O_AT)
        d = t - (LINE - 1)

        @pl.when(t == 0)
        def _():
            arrived(chip)
            vis = aux[:, 2 * HD:3 * HD]
            visible = jnp.concatenate([
                jnp.concatenate([vis[:tok], jnp.zeros_like(vis[:tok])], axis=1),
                jnp.concatenate([jnp.ones_like(vis[tok:]), vis[tok:]], axis=1)], axis=0) > 0.5
            attend(qs, m_ref, l_ref, acc, block(0, chip, 1), block(1, chip, 1), visible)

        @pl.when(d == 0)
        def _():
            def one(z, _):
                slot = p.y * LINE + z
                pl.when(z != p.z)(lambda: arrived(slot))
                pl.when(z < p.z)(lambda: attend(qs, m_ref, l_ref, acc, block(0, slot, 1), block(1, slot, 1)))
                return 0
            lax.fori_loop(0, LINE, one, 0)

        def use(g, _):
            @pl.when((g >= 1) & (g < ROWS))
            def _():
                row = g_kv.row(g)
                start = pl.multiple_of(row * LINE, LINE)
                for i in range(LINE):
                    arrived(start + i)
                pl.when(row < p.y)(lambda: attend(qs, m_ref, l_ref, acc, block(0, start, LINE), block(1, start, LINE)))
            return 0

        @pl.when(d >= 1)
        def _():
            lax.fori_loop(2 * d - 1, 2 * d + 1, use, 0)
        return 0

    lax.fori_loop(0, WAVES, look, 0)

    done = (acc[...] / l_ref[...]).astype(jnp.bfloat16)
    share = tok // 8
    for h in range(2):
        for xt in range(4):
            for zt in range(2):
                for c in range(2):
                    src = h * 2 * tok + c * tok + (zt * 4 + xt) * share
                    dst = (xt * 4 + zt * 2 + c) * share
                    att[core, dst:dst + share, h * HD:(h + 1) * HD] = done[src:src + share]
    swap = remote(att.at[core], att.at[core], att_sem.at[0], att_sem.at[1], sib)
    swap.start()
    swap.wait()

    span = LINE * 64
    piece = 4 * share
    wide_chunk = 2 * span

    def x_copies(c):
        cols = pl.ds(pl.multiple_of(c * wide_chunk, wide_chunk), wide_chunk)
        out = []
        for k, step in enumerate((1, 3, 2)):
            to = (p.x + step) % 4
            out.append(remote(part.at[to, :, cols], xin.at[k, :, cols], x_s.at[k, c], x_r.at[k, c], p.across(step)))
        return out

    def z_copy(c):
        cols = pl.ds(pl.multiple_of(c * wide_chunk, wide_chunk), wide_chunk)
        return remote(zout.at[:, cols], zin.at[:, cols], z_s.at[c], z_r.at[c], p.far())

    def t_copy(c):
        cols = pl.ds(pl.multiple_of(c * wide_chunk, wide_chunk), wide_chunk)
        return remote(fin.at[1 - core, :, cols], tin.at[:, cols], t_s.at[c], t_r.at[c], sib)

    def produce(c, _):
        for half in range(2):
            r = 2 * c + half
            at = pl.ds(pl.multiple_of(r * LINE, LINE), LINE)
            nt = (((1,), (1,)), ((), ()))
            left = jnp.concatenate([att[0], att[1]], axis=1)
            prod = lax.dot_general(left[:, :wide], of[at].reshape(span, wide), nt, preferred_element_type=jnp.float32)
            prod += lax.dot_general(left[:, wide:], ol[at].reshape(span, ol.shape[2]), nt, preferred_element_type=jnp.float32)
            part[:, :, pl.ds(pl.multiple_of(r * span, span), span)] = prod.astype(jnp.bfloat16).reshape(4, piece, span)
        for cp in x_copies(c):
            cp.start()
        return 0

    lax.fori_loop(0, ROWS // 2, produce, 0)

    def merge_x(c, _):
        cols = pl.ds(pl.multiple_of(c * wide_chunk, wide_chunk), wide_chunk)
        for cp in x_copies(c):
            cp.wait_recv()
        half = piece // 2

        def summed(z):
            at = pl.ds(pl.multiple_of(z * half, half), half)
            f = lambda v: v.astype(jnp.float32)
            return f(part[p.x, at, cols]) + f(xin[0, at, cols]) + f(xin[1, at, cols]) + f(xin[2, at, cols])

        zout[:, cols] = summed(1 - p.zh).astype(jnp.bfloat16)
        z_copy(c).start()
        fin[:, :, cols] = summed(p.zh).reshape(2, share, wide_chunk)
        return 0

    lax.fori_loop(0, ROWS // 2, merge_x, 0)

    def merge_z(c, _):
        cols = pl.ds(pl.multiple_of(c * wide_chunk, wide_chunk), wide_chunk)
        z_copy(c).wait_recv()
        fin[:, :, cols] += zin[:, cols].astype(jnp.float32).reshape(2, share, wide_chunk)
        t_copy(c).start()
        return 0

    lax.fori_loop(0, ROWS // 2, merge_z, 0)

    def merge_t(c, _):
        t_copy(c).wait_recv()
        return 0

    lax.fori_loop(0, ROWS // 2, merge_t, 0)
    mine, theirs = fin[core], tin[...]
    even = jnp.where(core == 0, mine, theirs)
    odd = jnp.where(core == 0, theirs, mine)
    low = lax.broadcasted_iota(jnp.int32, (share, HD), 1) < HD // 2
    at = pl.ds(pl.multiple_of(core * tok + p.head * share, share), share)
    square = jnp.zeros((share, 1), jnp.float32)
    tiles = []
    for m in range(CHIPS // 2):
        a, b = even[:, m * HD:(m + 1) * HD], odd[:, m * HD:(m + 1) * HD]
        pair = (jnp.where(low, a, pltpu.roll(b, 64, 1)), jnp.where(low, pltpu.roll(a, 64, 1), b))
        for k in range(2):
            cols = pl.ds((2 * m + k) * HD, HD)
            value = pair[k] + hid[at, cols].astype(jnp.float32)
            square += jnp.sum(value * value, axis=1, keepdims=True)
            tiles.append(value)
    norm = lax.rsqrt(square * (1.0 / (CHIPS * HD)) + 1e-05)
    for m in range(CHIPS):
        cols = pl.ds(m * HD, HD)
        out_ref[:, cols] = (tiles[m] * norm * gain_ref[:, cols]).astype(jnp.bfloat16)

    g_w.drain()
    g_o.drain()
    g_kv.drain()

    def rest(c, _):
        for cp in x_copies(c):
            cp.wait_send()
        z_copy(c).wait_send()
        t_copy(c).wait_send()
        return 0

    lax.fori_loop(0, ROWS // 2, rest, 0)

    def relays(slot, _):
        for part_at in range(2):
            relay(part_at, slot).wait_send()
        return 0

    lax.fori_loop(0, CHIPS, relays, 0)


def whole(x, wq, wk, wv, wo, aux, gain):
    tok = x.shape[0]
    width = x.shape[1]
    dma = pltpu.SemaphoreType.DMA
    anyspec = pl.BlockSpec(memory_space=pl.ANY)
    vm = pl.BlockSpec(memory_space=pltpu.VMEM)
    bf, f32 = jnp.bfloat16, jnp.float32
    share = tok // 8
    half = width // 2
    return pl.pallas_call(
        block_kernel,
        out_shape=jax.ShapeDtypeStruct((share, width), bf),
        in_specs=[anyspec] * 6 + [vm],
        out_specs=vm,
        scratch_shapes=[
            pltpu.VMEM((2 * tok, width), bf),
            pltpu.VMEM((2 * tok, aux.shape[1]), f32),
            pltpu.VMEM((CHIPS, 128, 256), bf),
            pltpu.VMEM((CHIPS, 128, 128), bf),
            pltpu.VMEM((2 * tok, 256), f32),
            pltpu.VMEM((2 * tok, 128), f32),
            pltpu.VMEM((2, CHIPS, 192, HD), bf),
            pltpu.VMEM((2, CHIPS, 64, HD), bf),
            pltpu.VMEM((CHIPS, 64, 384), bf),
            pltpu.VMEM((CHIPS, 64, 128), bf),
            pltpu.VMEM((4 * tok, HD), bf),
            pltpu.VMEM((4 * tok, 1), f32),
            pltpu.VMEM((4 * tok, 1), f32),
            pltpu.VMEM((4 * tok, HD), f32),
            pltpu.VMEM((2, 2 * tok, 256), bf),
            pltpu.VMEM((4, 4 * share, half), bf),
            pltpu.VMEM((3, 4 * share, half), bf),
            pltpu.VMEM((2 * share, half), bf),
            pltpu.VMEM((2 * share, half), bf),
            pltpu.VMEM((2, share, half), f32),
            pltpu.VMEM((share, half), f32),
            dma((6,)), dma((4,)), dma((4,)),
            dma((2, CHIPS)), dma((2, CHIPS)), dma((2,)),
            dma((3, 4)), dma((3, 4)), dma((4,)), dma((4,)), dma((4,)), dma((4,)),
        ] + Gather.scratch() * 3,
        compiler_params=pltpu.CompilerParams(collective_id=0, has_side_effects=True, vmem_limit_bytes=56 << 20),
        name="block",
    )(x, wq, wk, wv, wo, aux, gain)


def on_device(hidden_in, positions, w_query, w_key, w_value, w_out, norm_gain):
    visible = (positions[None, :] <= positions[:, None]).astype(jnp.float32)
    aux = jnp.concatenate([angles(positions), visible], axis=1)
    return whole(hidden_in, w_query, w_key, w_value, w_out.T, aux, norm_gain.reshape(1, -1))


def solution(mesh):
    return jax.shard_map(
        on_device,
        mesh=mesh,
        in_specs=(P("ctx", None), P("ctx"), P("ctx", "head"), P("ctx", "head"), P("ctx", "head"), P("head", "ctx"), P()),
        out_specs=P(("ctx", "head"), None),
        check_vma=False,
    )
```

time: 490 us -> 123 us (0.25)
  waiting for transfers between devices: 434 us -> 0 us
  Pallas kernels: 0 us -> 119 us
  matrix products: 26.8 us -> 0 us
  other arithmetic: 14.3 us -> 0.41 us
  between operations: 13.2 us -> 0.03 us
    all_gather x3 -> x0, waiting for transfers between devices: 344 us -> none  [the longest x1 130 us: on_device(): w_all = lax.all_gather(joined, 'ctx', axis=0, tiled=True)]
    pallas_call x0 -> x1, Pallas kernels: none -> 119 us  [whole(): pl.pallas_call(block_kernel, out_shape=jax.ShapeDtypeStruct((share, width...]
    reduce_scatter x1 -> x0, waiting for transfers between devices: 88.9 us -> none  [on_device(): lax.psum_scatter(product, 'head', scatter_dimension=0, tiled=True)]
    dot_general x4 -> x0, matrix products: 26.8 us -> none  [the longest x1 8.93 us: on_device(): jnp.einsum('rd,kd->rk', rows, keys, preferred_element_type=jnp.float32)]
    reduce_sum x2 -> x0, other arithmetic: 9.42 us -> none  [the longest x1 8.3 us: on_device(): total = jnp.sum(weight, axis=-1, keepdims=True)]
  transfers between devices with their start and end apart: 4 -> 0, of which waited for: 4 -> 0; matrix products, arithmetic and copies ran while one was open for 6% -> 0% of each run, Pallas kernels for 0% -> 0%
where the time goes in v2:
time: 123 us
  Pallas kernels  119 us (97%)
  local copies, waits for them, and re-layouts  2.99 us (2%)
    pallas_call x1, Pallas kernels, whole(): pl.pallas_call(block_kernel, out_shape=jax.ShapeDtypeStruct((share, width...  119 us

profile of v2, /device:TPU:1, one launch (start us, length us, event | category | flops | bytes accessed | tf_op | source)
XLA Modules:
  0.0 122.8 jit_solution(6156200773309394844)
XLA Ops:
  0.0 0.0 copy-start
  0.0 0.7 copy-done
  0.7 0.1 compare_convert_fusion
  0.8 0.3 multiply_sine_fusion
  1.1 0.8 concatenate.3.aux_ref
  1.8 119.3 %block.1 = bf16[16,4096]{1,0:T(8,128)(2,1)} custom-call(bf16[128,4096]{1,0:T(8,128)(2,1)} %x_ref.1, bf16[64,512]{1,0:T(8,128)(2,1)} %wq_ref.1, bf16[64,128]{1,0:T(8,128)(2,1)} %wk_ref.1, bf16[64,128]{1,0:T(8,128)(2,1)} %wv_ref.1, bf16[64,512]{1,0:T(8,128)(2,1)} %bitcast.2, f32[128,384]{1,0:T(8,128)} %concatenate.3.aux_ref, f32[1,4096]{1,0:T(1,128)} %bitcast.3), custom_call_target="tpu_custom_call" | custom-call | tf_op jit(solution)/shard_map/block/pallas_call | solution.py:510
  121.2 1.6 %copy.10 = bf16[16,4096]{1,0:T(8,128)(2,1)} copy(bf16[16,4096]{1,0:T(8,128)(2,1)} %block.1) | data formatting | bytes 262144
  (2 shorter events, 0.0 us)
Async XLA Ops:
  0.0 0.7 copy-start

commit v3 on v2

v3 whole, which is shorter than its diff:
```python
import jax
import jax.numpy as jnp
from jax import lax
from jax.experimental import pallas as pl
from jax.experimental.pallas import tpu as pltpu
from jax.sharding import PartitionSpec as P

MESH = pl.DeviceIdType.MESH
HD = 128
ROWS = 8
LINE = 4
CHIPS = ROWS * LINE
ROUNDS = ROWS // 2 + 2
USE_AT = 2
STEPS = ROUNDS + USE_AT - 1
O_BEGIN = 0
O_PLAN = ((6, 1), (12, 2), (13, 3), (14, 4), (15, 5))
MERGE_AT = 2
NEGATIVE = -1e30
SCALE = 1.4426950408889634 / HD ** 0.5


class Place:
    def __init__(self):
        ctx = lax.axis_index("ctx")
        head = lax.axis_index("head")
        self.core = ctx % 2
        self.z = (ctx // 2) % LINE
        self.y = ctx // (2 * LINE)
        self.x = head % 4
        self.zh = head // 4
        self.chip = ctx // 2
        self.ctx = ctx
        self.head = head

    def at(self, y, z, core):
        return ((y * LINE + z) * 2 + core, self.head)

    def sibling(self):
        return (self.chip * 2 + 1 - self.core, self.head)

    def up(self):
        return self.at((self.y + 1) % ROWS, self.z, self.core)

    def down(self):
        return self.at((self.y + ROWS - 1) % ROWS, self.z, self.core)

    def across(self, steps):
        return (self.ctx, self.zh * 4 + (self.x + 4 + steps) % 4)

    def far(self, core):
        return (self.chip * 2 + core, (1 - self.zh) * 4 + self.x)

    def order(self, i):
        z = self.z
        if i == 0:
            return z
        a = (1, 0, 3, 2)
        b = (2, 2, 1, 1)
        c = (3, 3, 0, 0)
        t = (a, b, c)[i - 1]
        return jnp.where(z == 0, t[0], jnp.where(z == 1, t[1], jnp.where(z == 2, t[2], t[3])))


class Gather:
    def __init__(self, place, buf, cut, sems):
        self.p = place
        self.buf, self.cut = buf, cut
        self.rf, self.ly, self.lz, self.out = sems

    @staticmethod
    def scratch():
        dma = pltpu.SemaphoreType.DMA
        return [dma((CHIPS,)), dma((ROWS,)), dma((ROWS,)), dma((1,))]

    def row(self, g):
        d = (g + 1) // 2
        up = jnp.logical_and(g % 2 == 1, jnp.logical_or(g < 7, self.p.core == 0))
        return jnp.where(up, self.p.y + ROWS - d, self.p.y + d) % ROWS

    def first(self, slot):
        return self.buf.at[slot, pl.ds(0, self.cut)]

    def last(self, slot):
        return self.buf.at[slot, pl.ds(self.cut, self.buf.shape[1] - self.cut)]

    def copy(self, ref, sem, device):
        return remote(ref, ref, self.out.at[0], sem, device)

    def onward(self, g):
        core = self.p.core
        return ((g == 1) | (g == 3) | ((g == 5) & (core == 0)),
                (g == 2) | (g == 4) | ((g == 6) & (core == 1)))

    def along(self, make, g):
        up, down = self.onward(g)

        @pl.when(up)
        def _():
            make(self.p.up()).start()

        @pl.when(down)
        def _():
            make(self.p.down()).start()

    def line(self, make):
        for i in range(1, LINE):
            make(self.p.at(self.p.y, self.p.order(i), self.p.core)).start()

    def begin(self):
        p = self.p
        slot = p.chip
        self.line(lambda dev: self.copy(self.first(slot), self.rf.at[slot], dev))
        for dev in (p.up(), p.down()):
            self.copy(self.last(slot), self.ly.at[p.y], dev).start()
            self.copy(self.first(slot), self.rf.at[slot], dev).start()
        self.line(lambda dev: self.copy(self.last(slot), self.lz.at[p.y], dev))

    def near(self, g):
        row = self.row(g)
        slot = row * LINE + self.p.z
        here = self.copy(self.last(slot), self.ly.at[row], self.p.up())
        here.wait_recv()
        self.along(lambda dev: self.copy(self.last(slot), self.ly.at[row], dev), g)
        self.line(lambda dev: self.copy(self.last(slot), self.lz.at[row], dev))
        self.pass_on(g, slot)

    def pass_on(self, g, slot):
        make = lambda dev: self.copy(self.first(slot), self.rf.at[slot], dev)
        make(self.p.up()).wait_recv()
        self.along(make, g)

    def others(self, g):
        row = self.row(g)
        for i in range(1, LINE):
            self.pass_on(g, row * LINE + self.p.order(i))

    def line_arrived(self, row):
        three = self.buf.at[pl.ds(0, LINE - 1), pl.ds(self.cut, self.buf.shape[1] - self.cut)]
        self.copy(three, self.lz.at[row], self.p.up()).wait_recv()

    def round(self, t):
        for g in (2 * t - 1, 2 * t):
            pl.when((g >= 1) & (g < ROWS))(lambda g=g: self.near(g))

        @pl.when(t == 1)
        def _():
            for i in range(1, LINE):
                slot = self.p.y * LINE + self.p.order(i)
                make = lambda dev: self.copy(self.first(slot), self.rf.at[slot], dev)
                make(self.p.up()).wait_recv()
                make(self.p.up()).start()
                make(self.p.down()).start()

        for g in (2 * t - 3, 2 * t - 2):
            pl.when((g >= 1) & (g < ROWS))(lambda g=g: self.others(g))

    def drain(self):
        sent = self.buf.at[pl.ds(0, CHIPS - 1)]
        self.copy(sent, self.ly.at[0], self.p.up()).wait_send()


def remote(src, dst, send, recv, device):
    return pltpu.make_async_remote_copy(
        src_ref=src, dst_ref=dst, send_sem=send, recv_sem=recv, device_id=device, device_id_type=MESH)


def entry(p):
    bar = pltpu.get_barrier_semaphore()
    devices = [p.far(p.core), p.far(1 - p.core), p.across(2)] + [p.at(p.y, p.order(i), p.core) for i in range(LINE - 1, 0, -1)]
    devices += [p.across(1), p.across(-1), p.up(), p.down(), p.sibling()]
    for d in devices:
        pl.semaphore_signal(bar, inc=1, device_id=d, device_id_type=MESH)
    pl.semaphore_wait(bar, len(devices))


def load_inputs(p, x_ref, wq_ref, wk_ref, wv_ref, aux_ref, hid, aux, wall, loc, snd, rcv):
    core, chip = p.core, p.chip
    tok = x_ref.shape[0]
    depth = wq_ref.shape[0]
    half = wq_ref.shape[1] // 2
    other = 1 - core
    mine = pl.ds(pl.multiple_of(core * half, half), half)
    theirs = pl.ds(pl.multiple_of(other * half, half), half)
    span = pl.ds(pl.multiple_of(core * depth, depth), depth)
    rows = pl.ds(pl.multiple_of(core * tok, tok), tok)
    sib = p.sibling()
    slot_f = wall.at[chip, span, pl.ds(0, half)]
    slot_l = wall.at[chip, span, pl.ds(half, HD)]
    rem = [
        remote(wq_ref.at[:, theirs], slot_f, snd.at[0], rcv.at[0], sib),
        None,
        remote(x_ref, hid.at[rows], snd.at[2], rcv.at[2], sib),
        remote(aux_ref, aux.at[rows], snd.at[3], rcv.at[3], sib),
    ]
    own = [
        pltpu.make_async_copy(wq_ref.at[:, mine], slot_f, loc.at[0]),
        None,
        pltpu.make_async_copy(x_ref, hid.at[rows], loc.at[2]),
        pltpu.make_async_copy(aux_ref, aux.at[rows], loc.at[3]),
    ]

    @pl.when(core == 0)
    def _():
        remote(wv_ref, slot_l, snd.at[1], rcv.at[1], sib).start()
        pltpu.make_async_copy(wk_ref, slot_l, loc.at[1]).start()

    @pl.when(core == 1)
    def _():
        remote(wk_ref, slot_l, snd.at[1], rcv.at[1], sib).start()
        pltpu.make_async_copy(wv_ref, slot_l, loc.at[1]).start()

    rem[1] = remote(wk_ref, slot_l, snd.at[1], rcv.at[1], sib)
    own[1] = pltpu.make_async_copy(wk_ref, slot_l, loc.at[1])
    for k in (0, 2, 3):
        rem[k].start()
        own[k].start()
    return rem, own


def wait_inputs(rem, own, ks):
    for k in ks:
        own[k].wait()
        rem[k].wait_send()
        rem[k].wait_recv()


def turn(u, cosine, sine):
    return u * cosine + pltpu.roll(u, 64, 1) * sine


def angles(positions):
    half = HD // 2
    inverse = 500000.0 ** (-(jnp.arange(half, dtype=jnp.float32) * 2.0 / HD))
    angle = positions.astype(jnp.float32)[:, None] * inverse[None, :]
    cosine, sine = jnp.cos(angle), jnp.sin(angle)
    return jnp.concatenate([cosine, cosine, -sine, sine], axis=1)

def attend(q_ref, m_ref, l_ref, acc_ref, keys, values, visible=None):
    rows = q_ref.shape[0] // 2
    for h in range(2):
        at = pl.ds(h * rows, rows)
        score = lax.dot_general(q_ref[at], keys, (((1,), (1,)), ((), ())), preferred_element_type=jnp.float32)
        if visible is not None:
            score = jnp.where(visible, score, NEGATIVE)
        before = m_ref[at]
        peak = jnp.maximum(before, jnp.max(score, axis=1, keepdims=True))
        fade = jnp.exp2((before - peak) * SCALE)
        weight = jnp.exp2((score - peak) * SCALE)
        m_ref[at] = peak
        l_ref[at] = l_ref[at] * fade + jnp.sum(weight, axis=1, keepdims=True)
        acc_ref[at] = acc_ref[at] * fade + jnp.dot(
            weight.astype(jnp.bfloat16), values, preferred_element_type=jnp.float32)


def planned(step):
    at = jnp.int32(-1)
    for when, what in O_PLAN:
        at = jnp.where(step == when, what, at)
    return at


def block_kernel(x_ref, wq_ref, wk_ref, wv_ref, wo_ref, aux_ref, gain_ref, out_ref,
                 hid, aux, wall, full, kv, oall, qs, m_ref, l_ref, acc, att,
                 part, xin, zout, zin, fin, tin, loc, snd, rcv, sib_s, sib_r, att_sem, x_s, x_r, z_s, z_r, t_s, t_r, *gsems):
    p = Place()
    core, chip = p.core, p.chip
    tok = x_ref.shape[0]
    sib = p.sibling()
    entry(p)
    rem, own = load_inputs(p, x_ref, wq_ref, wk_ref, wv_ref, aux_ref, hid, aux, wall, loc, snd, rcv)
    o_own = pltpu.make_async_copy(wo_ref, oall.at[chip], loc.at[4])
    o_own.start()
    n = len(gsems) // 3
    g_w = Gather(p, wall, 96, gsems[:n])
    g_o = Gather(p, oall, 48, gsems[n:2 * n])
    g_kv = Gather(p, kv.at[core], 192, gsems[2 * n:])
    wait_inputs(rem, own, (0, 1))
    g_w.begin()
    full[...] = jnp.zeros_like(full)

    def project(t, _):
        g_w.round(t)
        @pl.when(t == O_BEGIN)
        def _():
            o_own.wait()
            g_o.begin()

        g_o.round(planned(t))
        d = t - USE_AT

        def use(g, _):
            @pl.when((g >= 0) & (g < ROWS))
            def _():
                row = g_w.row(g)
                g_w.line_arrived(row)
                depth = LINE * 128
                left = hid[:, pl.ds(pl.multiple_of(row * depth, depth), depth)]
                at = pl.ds(pl.multiple_of(row * LINE, LINE), LINE)
                full[...] += jnp.dot(left, wall[at].reshape(depth, wall.shape[2]), preferred_element_type=jnp.float32)
            return 0

        @pl.when(d == 0)
        def _():
            wait_inputs(rem, own, (2, 3))

        @pl.when(d >= 0)
        def _():
            lax.fori_loop(2 * d - 1, 2 * d + 1, use, 0)
        return 0

    lax.fori_loop(0, STEPS, project, 0)

    cosine, sine = aux[:, 0:HD], aux[:, HD:2 * HD]
    last = full[:, 2 * HD:]
    kv[core, chip] = jnp.where(core == 0, turn(last, cosine, sine), last).astype(jnp.bfloat16)
    def relay(slots, sem, kind):
        ref = kv.at[kind, slots]
        return remote(ref, ref, sib_s.at[0], sib_r.at[sem], sib)

    relay(pl.ds(chip, 1), ROWS, core).start()
    g_kv.begin()
    for h in range(2):
        qs[pl.ds(2 * tok * h, 2 * tok)] = turn(full[:, h * HD:(h + 1) * HD], cosine, sine).astype(jnp.bfloat16)
    m_ref[...] = jnp.full_like(m_ref, NEGATIVE)
    l_ref[...] = jnp.zeros_like(l_ref)
    acc[...] = jnp.zeros_like(acc)

    def block(kind, start, count):
        return kv[kind, pl.ds(start, count)].reshape(count * 2 * tok, HD)

    def look(t, _):
        g_kv.round(t)
        g_o.round(planned(t + STEPS))
        d = t - USE_AT

        @pl.when(t == 0)
        def _():
            relay(pl.ds(chip, 1), ROWS, 1 - core).wait_recv()
            vis = aux[:, 2 * HD:3 * HD]
            visible = jnp.concatenate([
                jnp.concatenate([vis[:tok], jnp.zeros_like(vis[:tok])], axis=1),
                jnp.concatenate([jnp.ones_like(vis[tok:]), vis[tok:]], axis=1)], axis=0) > 0.5
            attend(qs, m_ref, l_ref, acc, block(0, chip, 1), block(1, chip, 1), visible)

        @pl.when(d == 0)
        def _():
            g_kv.line_arrived(p.y)
            for i in range(1, LINE):
                relay(pl.ds(p.y * LINE + p.order(i), 1), p.y, core).start()
            relay(pl.ds(0, LINE - 1), p.y, 1 - core).wait_recv()

            def one(z, _):
                slot = p.y * LINE + z
                attend(qs, m_ref, l_ref, acc, block(0, slot, 1), block(1, slot, 1))
                return 0
            lax.fori_loop(0, p.z, one, 0)

        def forward(g, _):
            @pl.when((g >= 1) & (g < ROWS))
            def _():
                row = g_kv.row(g)
                g_kv.line_arrived(row)
                relay(pl.ds(pl.multiple_of(row * LINE, LINE), LINE), row, core).start()
            return 0

        def use(g, _):
            @pl.when((g >= 1) & (g < ROWS))
            def _():
                row = g_kv.row(g)
                start = pl.multiple_of(row * LINE, LINE)
                relay(pl.ds(start, LINE), row, 1 - core).wait_recv()
                pl.when(row < p.y)(lambda: attend(qs, m_ref, l_ref, acc, block(0, start, LINE), block(1, start, LINE)))
            return 0

        @pl.when(d >= 1)
        def _():
            lax.fori_loop(2 * d - 1, 2 * d + 1, forward, 0)
            lax.fori_loop(2 * d - 1, 2 * d + 1, use, 0)
        return 0

    lax.fori_loop(0, STEPS, look, 0)

    done = (acc[...] / l_ref[...]).astype(jnp.bfloat16)
    share = tok // 8
    for h in range(2):
        for xt in range(4):
            for zt in range(2):
                for c in range(2):
                    src = h * 2 * tok + c * tok + (zt * 4 + xt) * share
                    dst = (xt * 4 + zt * 2 + c) * share
                    att[core, dst:dst + share, h * HD:(h + 1) * HD] = done[src:src + share]
    swap = remote(att.at[core], att.at[core], att_sem.at[0], att_sem.at[1], sib)
    swap.start()
    swap.wait()

    span = LINE * 64
    piece = 4 * share
    wide_chunk = 2 * span

    def x_copies(c):
        cols = pl.ds(pl.multiple_of(c * wide_chunk, wide_chunk), wide_chunk)
        return [remote(part.at[(p.x + step) % 4, :, cols], xin.at[k, :, cols], x_s.at[0], x_r.at[k, c], p.across(step))
                for k, step in enumerate((2, 1, 3))]

    def keep(which):
        return pl.ds(pl.multiple_of(which * share, share), share)

    def z_copy(cols, to):
        return remote(zout.at[keep(to), cols], zin.at[core, :, cols], z_s.at[0], z_r.at[core], p.far(to))

    def t_copy(cols):
        return remote(fin.at[1 - core, :, cols], tin.at[:, cols], t_s.at[0], t_r.at[0], sib)

    def produce(c):
        for half in range(2):
            g = 2 * c + half
            r = g_o.row(g)
            at = pl.ds(pl.multiple_of(r * LINE, LINE), LINE)
            g_o.line_arrived(r)
            left = jnp.concatenate([att[0], att[1]], axis=1)
            prod = lax.dot_general(left, oall[at].reshape(span, oall.shape[2]), (((1,), (1,)), ((), ())),
                                   preferred_element_type=jnp.float32)
            part[:, :, pl.ds(pl.multiple_of(g * span, span), span)] = prod.astype(jnp.bfloat16).reshape(4, piece, span)
        for cp in x_copies(c):
            cp.start()

    def merge(c):
        cols = pl.ds(pl.multiple_of(c * wide_chunk, wide_chunk), wide_chunk)
        for cp in x_copies(c):
            cp.wait_recv()
        half = piece // 2

        def summed(z):
            at = pl.ds(pl.multiple_of(z * half, half), half)
            f = lambda v: v.astype(jnp.float32)
            return f(part[p.x, at, cols]) + f(xin[0, at, cols]) + f(xin[1, at, cols]) + f(xin[2, at, cols])

        zout[:, cols] = summed(1 - p.zh).astype(jnp.bfloat16)
        z_copy(cols, core).start()
        z_copy(cols, 1 - core).start()
        fin[:, :, cols] = summed(p.zh).reshape(2, share, wide_chunk)
        t_copy(cols).start()

    chunks = ROWS // 2

    def flow(s, _):
        pl.when(s < chunks)(lambda: produce(s))
        g_o.round(planned(s + 2 * STEPS))
        pl.when(s >= MERGE_AT)(lambda: merge(s - MERGE_AT))
        return 0

    lax.fori_loop(0, chunks + MERGE_AT, flow, 0)
    remote(tin, tin, t_s.at[0], t_r.at[0], sib).wait_recv()
    for k in range(2):
        remote(zin.at[k], zin.at[k], z_s.at[0], z_r.at[k], sib).wait_recv()
    mine = fin[core] + zin[core].astype(jnp.float32)
    theirs = tin[...] + zin[1 - core].astype(jnp.float32)
    even = jnp.where(core == 0, mine, theirs)
    odd = jnp.where(core == 0, theirs, mine)
    low = lax.broadcasted_iota(jnp.int32, (share, HD), 1) < HD // 2
    at = pl.ds(pl.multiple_of(core * tok + p.head * share, share), share)
    square = jnp.zeros((share, 1), jnp.float32)
    tiles = []
    for g in range(ROWS):
        for m in range(2):
            cut = g * span + m * HD
            a, b = even[:, cut:cut + HD], odd[:, cut:cut + HD]
            pair = (jnp.where(low, a, pltpu.roll(b, 64, 1)), jnp.where(low, pltpu.roll(a, 64, 1), b))
            for k in range(2):
                cols = pl.ds(pl.multiple_of(g_o.row(g) * 2 * span + (2 * m + k) * HD, HD), HD)
                value = pair[k] + hid[at, cols].astype(jnp.float32)
                square += jnp.sum(value * value, axis=1, keepdims=True)
                tiles.append((cols, value))
    norm = lax.rsqrt(square * (1.0 / (CHIPS * HD)) + 1e-05)
    for cols, value in tiles:
        out_ref[:, cols] = (value * norm * gain_ref[:, cols]).astype(jnp.bfloat16)

    g_w.drain()
    g_o.drain()
    g_kv.drain()

    remote(xin, xin, x_s.at[0], x_r.at[0, 0], p.across(1)).wait_send()

    remote(zout, zout, z_s.at[0], z_r.at[0], sib).wait_send()
    remote(tin, tin, t_s.at[0], t_r.at[0], sib).wait_send()
    relay(pl.ds(0, CHIPS), 0, core).wait_send()


def whole(x, wq, wk, wv, wo, aux, gain):
    tok = x.shape[0]
    width = x.shape[1]
    dma = pltpu.SemaphoreType.DMA
    anyspec = pl.BlockSpec(memory_space=pl.ANY)
    vm = pl.BlockSpec(memory_space=pltpu.VMEM)
    bf, f32 = jnp.bfloat16, jnp.float32
    share = tok // 8
    half = width // 2
    return pl.pallas_call(
        block_kernel,
        out_shape=jax.ShapeDtypeStruct((share, width), bf),
        in_specs=[anyspec] * 6 + [vm],
        out_specs=vm,
        scratch_shapes=[
            pltpu.VMEM((2 * tok, width), bf),
            pltpu.VMEM((2 * tok, aux.shape[1]), f32),
            pltpu.VMEM((CHIPS, 128, 384), bf),
            pltpu.VMEM((2 * tok, 384), f32),
            pltpu.VMEM((2, CHIPS, 2 * tok, HD), bf),
            pltpu.VMEM((CHIPS, 64, 512), bf),
            pltpu.VMEM((4 * tok, HD), bf),
            pltpu.VMEM((4 * tok, 1), f32),
            pltpu.VMEM((4 * tok, 1), f32),
            pltpu.VMEM((4 * tok, HD), f32),
            pltpu.VMEM((2, 2 * tok, 256), bf),
            pltpu.VMEM((4, 4 * share, half), bf),
            pltpu.VMEM((3, 4 * share, half), bf),
            pltpu.VMEM((2 * share, half), bf),
            pltpu.VMEM((2, share, half), bf),
            pltpu.VMEM((2, share, half), f32),
            pltpu.VMEM((share, half), f32),
            dma((5,)), dma((4,)), dma((4,)),
            dma((1,)), dma((ROWS + 1,)), dma((2,)),
            dma((1,)), dma((3, 4)), dma((1,)), dma((2,)), dma((1,)), dma((1,)),
        ] + Gather.scratch() * 3,
        compiler_params=pltpu.CompilerParams(collective_id=0, has_side_effects=True, vmem_limit_bytes=56 << 20),
        name="block",
    )(x, wq, wk, wv, wo, aux, gain)


def on_device(hidden_in, positions, w_query, w_key, w_value, w_out, norm_gain):
    visible = (positions[None, :] <= positions[:, None]).astype(jnp.float32)
    aux = jnp.concatenate([angles(positions), visible], axis=1)
    return whole(hidden_in, w_query, w_key, w_value, w_out.T, aux, norm_gain.reshape(1, -1))


def solution(mesh):
    return jax.shard_map(
        on_device,
        mesh=mesh,
        in_specs=(P("ctx", None), P("ctx"), P("ctx", "head"), P("ctx", "head"), P("ctx", "head"), P("head", "ctx"), P()),
        out_specs=P(("ctx", "head"), None),
        check_vma=False,
    )
```

time: 123 us -> 112 us (0.911)
  Pallas kernels: 119 us -> 108 us
    pallas_call x1, Pallas kernels: 119 us -> 108 us  [whole(): pl.pallas_call(block_kernel, out_shape=jax.ShapeDtypeStruct((share, width...]
where the time goes in v3:
time: 112 us
  Pallas kernels  108 us (96%)
  local copies, waits for them, and re-layouts  2.99 us (3%)
    pallas_call x1, Pallas kernels, whole(): pl.pallas_call(block_kernel, out_shape=jax.ShapeDtypeStruct((share, width...  108 us

profile of v3, /device:TPU:1, one launch (start us, length us, event | category | flops | bytes accessed | tf_op | source)
XLA Modules:
  0.0 111.5 jit_solution(13575577322281316120)
XLA Ops:
  0.0 0.0 copy-start
  0.0 0.7 copy-done
  0.7 0.1 compare_convert_fusion
  0.8 0.3 multiply_sine_fusion
  1.1 0.8 concatenate.3.aux_ref
  1.8 108.1 %block.1 = bf16[16,4096]{1,0:T(8,128)(2,1)} custom-call(bf16[128,4096]{1,0:T(8,128)(2,1)} %x_ref.1, bf16[64,512]{1,0:T(8,128)(2,1)} %wq_ref.1, bf16[64,128]{1,0:T(8,128)(2,1)} %wk_ref.1, bf16[64,128]{1,0:T(8,128)(2,1)} %wv_ref.1, bf16[64,512]{1,0:T(8,128)(2,1)} %bitcast.2, f32[128,384]{1,0:T(8,128)} %concatenate.3.aux_ref, f32[1,4096]{1,0:T(1,128)} %bitcast.3), custom_call_target="tpu_custom_call" | custom-call | tf_op jit(solution)/shard_map/block/pallas_call | solution.py:499
  109.9 1.6 %copy.10 = bf16[16,4096]{1,0:T(8,128)(2,1)} copy(bf16[16,4096]{1,0:T(8,128)(2,1)} %block.1) | data formatting | bytes 262144
  (2 shorter events, 0.0 us)
Async XLA Ops:
  0.0 0.7 copy-start

commit v4 on v3

--- a/solution.py
+++ b/solution.py
@@ -4,6 +4,7 @@
 from jax.experimental import pallas as pl
 from jax.experimental.pallas import tpu as pltpu
 from jax.sharding import PartitionSpec as P
+import numpy as np
 
 MESH = pl.DeviceIdType.MESH
 HD = 128
@@ -14,8 +15,8 @@
 USE_AT = 2
 STEPS = ROUNDS + USE_AT - 1
 O_BEGIN = 0
-O_PLAN = ((6, 1), (12, 2), (13, 3), (14, 4), (15, 5))
-MERGE_AT = 2
+O_PLAN = ((5, 1), (12, 2), (13, 3), (15, 4), (17, 5))
+MERGE_AT = 3
 NEGATIVE = -1e30
 SCALE = 1.4426950408889634 / HD ** 0.5
 
@@ -174,67 +175,45 @@
     pl.semaphore_wait(bar, len(devices))
 
 
-def load_inputs(p, x_ref, wq_ref, wk_ref, wv_ref, aux_ref, hid, aux, wall, loc, snd, rcv):
-    core, chip = p.core, p.chip
-    tok = x_ref.shape[0]
-    depth = wq_ref.shape[0]
-    half = wq_ref.shape[1] // 2
-    other = 1 - core
-    mine = pl.ds(pl.multiple_of(core * half, half), half)
-    theirs = pl.ds(pl.multiple_of(other * half, half), half)
-    span = pl.ds(pl.multiple_of(core * depth, depth), depth)
-    rows = pl.ds(pl.multiple_of(core * tok, tok), tok)
-    sib = p.sibling()
-    slot_f = wall.at[chip, span, pl.ds(0, half)]
-    slot_l = wall.at[chip, span, pl.ds(half, HD)]
-    rem = [
-        remote(wq_ref.at[:, theirs], slot_f, snd.at[0], rcv.at[0], sib),
-        None,
-        remote(x_ref, hid.at[rows], snd.at[2], rcv.at[2], sib),
-        remote(aux_ref, aux.at[rows], snd.at[3], rcv.at[3], sib),
-    ]
-    own = [
-        pltpu.make_async_copy(wq_ref.at[:, mine], slot_f, loc.at[0]),
-        None,
-        pltpu.make_async_copy(x_ref, hid.at[rows], loc.at[2]),
-        pltpu.make_async_copy(aux_ref, aux.at[rows], loc.at[3]),
-    ]
-
-    @pl.when(core == 0)
-    def _():
-        remote(wv_ref, slot_l, snd.at[1], rcv.at[1], sib).start()
-        pltpu.make_async_copy(wk_ref, slot_l, loc.at[1]).start()
-
-    @pl.when(core == 1)
-    def _():
-        remote(wk_ref, slot_l, snd.at[1], rcv.at[1], sib).start()
-        pltpu.make_async_copy(wv_ref, slot_l, loc.at[1]).start()
-
-    rem[1] = remote(wk_ref, slot_l, snd.at[1], rcv.at[1], sib)
-    own[1] = pltpu.make_async_copy(wk_ref, slot_l, loc.at[1])
-    for k in (0, 2, 3):
-        rem[k].start()
-        own[k].start()
-    return rem, own
-
-
-def wait_inputs(rem, own, ks):
-    for k in ks:
-        own[k].wait()
-        rem[k].wait_send()
-        rem[k].wait_recv()
+class Inputs:
+    def __init__(self, p, x_ref, wq_ref, wk_ref, wv_ref, pos_ref, hid, pos, wall, loc, snd, rcv):
+        core = p.core
+        tok = x_ref.shape[0]
+        depth = wq_ref.shape[0]
+        half = wq_ref.shape[1] // 2
+        columns = lambda c: pl.ds(pl.multiple_of(c * half, half), half)
+        span = pl.ds(pl.multiple_of(core * depth, depth), depth)
+        rows = pl.ds(pl.multiple_of(core * tok, tok), tok)
+        slot_q = wall.at[p.chip, span, pl.ds(0, half)]
+        slot_l = wall.at[p.chip, span, pl.ds(half, HD)]
+        self.core = core
+        self.narrow = (wk_ref, wv_ref)
+        self.local = lambda ref, dst, k: pltpu.make_async_copy(ref, dst, loc.at[k])
+        self.cross = lambda ref, dst, k: remote(ref, dst, snd.at[k], rcv.at[k], p.sibling())
+        self.slot_l = slot_l
+        pairs = ((wq_ref.at[:, columns(core)], wq_ref.at[:, columns(1 - core)], slot_q), None,
+                 (x_ref, x_ref, hid.at[rows]), (pos_ref, pos_ref, pos.at[core]))
+        self.own = [self.local(q[0], q[2], k) if q else self.local(wk_ref, slot_l, 1) for k, q in enumerate(pairs)]
+        self.sent = [self.cross(q[1], q[2], k) if q else self.cross(wk_ref, slot_l, 1) for k, q in enumerate(pairs)]
+
+    def start(self, far):
+        make = self.cross if far else self.local
+        for c in range(2):
+            kept = self.narrow[1 - c if far else c]
+            pl.when(self.core == c)(lambda kept=kept: make(kept, self.slot_l, 1).start())
+        for k in (0, 3, 2):
+            (self.sent if far else self.own)[k].start()
+
+    def wait(self, *ks):
+        for k in ks:
+            self.own[k].wait()
+            self.sent[k].wait_send()
+            self.sent[k].wait_recv()
 
 
 def turn(u, cosine, sine):
     return u * cosine + pltpu.roll(u, 64, 1) * sine
 
-
-def angles(positions):
-    half = HD // 2
-    inverse = 500000.0 ** (-(jnp.arange(half, dtype=jnp.float32) * 2.0 / HD))
-    angle = positions.astype(jnp.float32)[:, None] * inverse[None, :]
-    cosine, sine = jnp.cos(angle), jnp.sin(angle)
-    return jnp.concatenate([cosine, cosine, -sine, sine], axis=1)
 
 def attend(q_ref, m_ref, l_ref, acc_ref, keys, values, visible=None):
     rows = q_ref.shape[0] // 2
@@ -260,24 +239,41 @@
     return at
 
 
-def block_kernel(x_ref, wq_ref, wk_ref, wv_ref, wo_ref, aux_ref, gain_ref, out_ref,
-                 hid, aux, wall, full, kv, oall, qs, m_ref, l_ref, acc, att,
+def block_kernel(x_ref, wq_ref, wk_ref, wv_ref, wo_ref, pos_ref, freq_ref, gain_ref, out_ref,
+                 hid, pos, freq, gain, aux, seen, wall, full, kv, oall, qs, m_ref, l_ref, acc, att,
                  part, xin, zout, zin, fin, tin, loc, snd, rcv, sib_s, sib_r, att_sem, x_s, x_r, z_s, z_r, t_s, t_r, *gsems):
     p = Place()
     core, chip = p.core, p.chip
     tok = x_ref.shape[0]
     sib = p.sibling()
+    given = Inputs(p, x_ref, wq_ref, wk_ref, wv_ref, pos_ref, hid, pos, wall, loc, snd, rcv)
+    o_own = pltpu.make_async_copy(wo_ref, oall.at[chip], loc.at[4])
+    f_own = pltpu.make_async_copy(freq_ref, freq, loc.at[5])
+    n_own = pltpu.make_async_copy(gain_ref, gain, loc.at[6])
+    given.start(False)
+    for c in (f_own, o_own, n_own):
+        c.start()
     entry(p)
-    rem, own = load_inputs(p, x_ref, wq_ref, wk_ref, wv_ref, aux_ref, hid, aux, wall, loc, snd, rcv)
-    o_own = pltpu.make_async_copy(wo_ref, oall.at[chip], loc.at[4])
-    o_own.start()
+    given.start(True)
     n = len(gsems) // 3
     g_w = Gather(p, wall, 96, gsems[:n])
     g_o = Gather(p, oall, 48, gsems[n:2 * n])
     g_kv = Gather(p, kv.at[core], 192, gsems[2 * n:])
-    wait_inputs(rem, own, (0, 1))
+    given.wait(0, 1)
     g_w.begin()
     full[...] = jnp.zeros_like(full)
+
+    given.wait(3)
+    f_own.wait()
+    sign = jnp.where(lax.broadcasted_iota(jnp.int32, (1, HD), 1) < HD // 2, -1.0, 1.0)
+    for c in range(2):
+        at = pl.ds(c * tok, tok)
+        column = jnp.transpose(jnp.broadcast_to(pos[c].astype(jnp.float32), (tok, tok)))
+        angle = column * freq[...]
+        aux[at, 0:HD] = jnp.cos(angle)
+        aux[at, HD:2 * HD] = jnp.sin(angle) * sign
+        for k in range(2):
+            seen[at, k * tok:(k + 1) * tok] = (pos[k].astype(jnp.float32) <= column).astype(jnp.float32)
 
     def project(t, _):
         g_w.round(t)
@@ -302,7 +298,7 @@
 
         @pl.when(d == 0)
         def _():
-            wait_inputs(rem, own, (2, 3))
+            given.wait(2)
 
         @pl.when(d >= 0)
         def _():
@@ -337,11 +333,7 @@
         @pl.when(t == 0)
         def _():
             relay(pl.ds(chip, 1), ROWS, 1 - core).wait_recv()
-            vis = aux[:, 2 * HD:3 * HD]
-            visible = jnp.concatenate([
-                jnp.concatenate([vis[:tok], jnp.zeros_like(vis[:tok])], axis=1),
-                jnp.concatenate([jnp.ones_like(vis[tok:]), vis[tok:]], axis=1)], axis=0) > 0.5
-            attend(qs, m_ref, l_ref, acc, block(0, chip, 1), block(1, chip, 1), visible)
+            attend(qs, m_ref, l_ref, acc, block(0, chip, 1), block(1, chip, 1), seen[...] > 0.5)
 
         @pl.when(d == 0)
         def _():
@@ -396,7 +388,7 @@
 
     span = LINE * 64
     piece = 4 * share
-    wide_chunk = 2 * span
+    wide_chunk = span
 
     def x_copies(c):
         cols = pl.ds(pl.multiple_of(c * wide_chunk, wide_chunk), wide_chunk)
@@ -412,17 +404,15 @@
     def t_copy(cols):
         return remote(fin.at[1 - core, :, cols], tin.at[:, cols], t_s.at[0], t_r.at[0], sib)
 
-    def produce(c):
-        for half in range(2):
-            g = 2 * c + half
-            r = g_o.row(g)
-            at = pl.ds(pl.multiple_of(r * LINE, LINE), LINE)
-            g_o.line_arrived(r)
-            left = jnp.concatenate([att[0], att[1]], axis=1)
-            prod = lax.dot_general(left, oall[at].reshape(span, oall.shape[2]), (((1,), (1,)), ((), ())),
-                                   preferred_element_type=jnp.float32)
-            part[:, :, pl.ds(pl.multiple_of(g * span, span), span)] = prod.astype(jnp.bfloat16).reshape(4, piece, span)
-        for cp in x_copies(c):
+    def produce(g):
+        r = g_o.row(g)
+        at = pl.ds(pl.multiple_of(r * LINE, LINE), LINE)
+        g_o.line_arrived(r)
+        left = jnp.concatenate([att[0], att[1]], axis=1)
+        prod = lax.dot_general(left, oall[at].reshape(span, oall.shape[2]), (((1,), (1,)), ((), ())),
+                               preferred_element_type=jnp.float32)
+        part[:, :, pl.ds(pl.multiple_of(g * span, span), span)] = prod.astype(jnp.bfloat16).reshape(4, piece, span)
+        for cp in x_copies(g):
             cp.start()
 
     def merge(c):
@@ -442,7 +432,7 @@
         fin[:, :, cols] = summed(p.zh).reshape(2, share, wide_chunk)
         t_copy(cols).start()
 
-    chunks = ROWS // 2
+    chunks = ROWS
 
     def flow(s, _):
         pl.when(s < chunks)(lambda: produce(s))
@@ -472,9 +462,10 @@
                 value = pair[k] + hid[at, cols].astype(jnp.float32)
                 square += jnp.sum(value * value, axis=1, keepdims=True)
                 tiles.append((cols, value))
+    n_own.wait()
     norm = lax.rsqrt(square * (1.0 / (CHIPS * HD)) + 1e-05)
     for cols, value in tiles:
-        out_ref[:, cols] = (value * norm * gain_ref[:, cols]).astype(jnp.bfloat16)
+        out_ref[:, cols] = (value * norm * gain[:, cols]).astype(jnp.bfloat16)
 
     g_w.drain()
     g_o.drain()
@@ -487,7 +478,7 @@
     relay(pl.ds(0, CHIPS), 0, core).wait_send()
 
 
-def whole(x, wq, wk, wv, wo, aux, gain):
+def whole(x, wq, wk, wv, wo, pos, freq, gain):
     tok = x.shape[0]
     width = x.shape[1]
     dma = pltpu.SemaphoreType.DMA
@@ -499,11 +490,15 @@
     return pl.pallas_call(
         block_kernel,
         out_shape=jax.ShapeDtypeStruct((share, width), bf),
-        in_specs=[anyspec] * 6 + [vm],
+        in_specs=[anyspec] * 8,
         out_specs=vm,
         scratch_shapes=[
             pltpu.VMEM((2 * tok, width), bf),
-            pltpu.VMEM((2 * tok, aux.shape[1]), f32),
+            pltpu.VMEM((2, 1, tok), jnp.int32),
+            pltpu.VMEM((1, HD), f32),
+            pltpu.VMEM((1, width), f32),
+            pltpu.VMEM((2 * tok, 2 * HD), f32),
+            pltpu.VMEM((2 * tok, 2 * tok), f32),
             pltpu.VMEM((CHIPS, 128, 384), bf),
             pltpu.VMEM((2 * tok, 384), f32),
             pltpu.VMEM((2, CHIPS, 2 * tok, HD), bf),
@@ -519,19 +514,19 @@
             pltpu.VMEM((2, share, half), bf),
             pltpu.VMEM((2, share, half), f32),
             pltpu.VMEM((share, half), f32),
-            dma((5,)), dma((4,)), dma((4,)),
+            dma((7,)), dma((4,)), dma((4,)),
             dma((1,)), dma((ROWS + 1,)), dma((2,)),
-            dma((1,)), dma((3, 4)), dma((1,)), dma((2,)), dma((1,)), dma((1,)),
+            dma((1,)), dma((3, ROWS)), dma((1,)), dma((2,)), dma((1,)), dma((1,)),
         ] + Gather.scratch() * 3,
         compiler_params=pltpu.CompilerParams(collective_id=0, has_side_effects=True, vmem_limit_bytes=56 << 20),
         name="block",
-    )(x, wq, wk, wv, wo, aux, gain)
+    )(x, wq, wk, wv, wo, pos, freq, gain)
 
 
 def on_device(hidden_in, positions, w_query, w_key, w_value, w_out, norm_gain):
-    visible = (positions[None, :] <= positions[:, None]).astype(jnp.float32)
-    aux = jnp.concatenate([angles(positions), visible], axis=1)
-    return whole(hidden_in, w_query, w_key, w_value, w_out.T, aux, norm_gain.reshape(1, -1))
+    half = np.arange(HD // 2, dtype=np.float64)
+    freq = jnp.asarray(np.tile(500000.0 ** (-2.0 * half / HD), 2).astype(np.float32).reshape(1, HD))
+    return whole(hidden_in, w_query, w_key, w_value, w_out.T, positions.reshape(1, -1), freq, norm_gain.reshape(1, -1))
 
 
 def solution(mesh):

time: 112 us -> 108 us (0.964)
  local copies, waits for them, and re-layouts: 2.99 us -> 1.57 us
    pallas_call x1, Pallas kernels: 108 us -> 107 us  [whole(): pl.pallas_call(block_kernel, out_shape=jax.ShapeDtypeStruct((share, width...]
where the time goes in v4:
time: 108 us
  Pallas kernels  107 us (99%)
  local copies, waits for them, and re-layouts  1.57 us (1%)
    pallas_call x1, Pallas kernels, whole(): pl.pallas_call(block_kernel, out_shape=jax.ShapeDtypeStruct((share, width...  107 us

profile of v4, /device:TPU:1, one launch (start us, length us, event | category | flops | bytes accessed | tf_op | source)
XLA Modules:
  0.0 108.1 jit_solution(17563089087440953530)
XLA Ops:
  0.0 106.5 %block.1 = bf16[16,4096]{1,0:T(8,128)(2,1)} custom-call(bf16[128,4096]{1,0:T(8,128)(2,1)} %x_ref.1, bf16[64,512]{1,0:T(8,128)(2,1)} %wq_ref.1, bf16[64,128]{1,0:T(8,128)(2,1)} %wk_ref.1, bf16[64,128]{1,0:T(8,128)(2,1)} %wv_ref.1, bf16[64,512]{1,0:T(8,128)(2,1)} %bitcast.3, s32[1,128]{1,0:T(1,128)} %bitcast.5, f32[1,128]{1,0:T(1,128)} %constant.2.clone.freq_ref, ...), custom_call_target="tpu_custom_call" | custom-call | tf_op jit(solution)/shard_map/block/pallas_call | solution.py:490
  106.5 1.6 %copy.10 = bf16[16,4096]{1,0:T(8,128)(2,1)} copy(bf16[16,4096]{1,0:T(8,128)(2,1)} %block.1) | data formatting | bytes 262144

commit v5 on v4

--- a/solution.py
+++ b/solution.py
@@ -15,7 +15,7 @@
 USE_AT = 2
 STEPS = ROUNDS + USE_AT - 1
 O_BEGIN = 0
-O_PLAN = ((5, 1), (12, 2), (13, 3), (15, 4), (17, 5))
+O_PLAN = ((4, 1), (12, 2), (13, 3), (14, 4), (16, 5))
 MERGE_AT = 3
 NEGATIVE = -1e30
 SCALE = 1.4426950408889634 / HD ** 0.5
@@ -276,7 +276,7 @@
             seen[at, k * tok:(k + 1) * tok] = (pos[k].astype(jnp.float32) <= column).astype(jnp.float32)
 
     def project(t, _):
-        g_w.round(t)
+        pl.when(t < ROUNDS - 1)(lambda: g_w.round(t))
         @pl.when(t == O_BEGIN)
         def _():
             o_own.wait()
@@ -303,6 +303,8 @@
         @pl.when(d >= 0)
         def _():
             lax.fori_loop(2 * d - 1, 2 * d + 1, use, 0)
+
+        pl.when(t == ROUNDS - 1)(lambda: g_w.others(ROWS - 1))
         return 0
 
     lax.fori_loop(0, STEPS, project, 0)
@@ -326,7 +328,7 @@
         return kv[kind, pl.ds(start, count)].reshape(count * 2 * tok, HD)
 
     def look(t, _):
-        g_kv.round(t)
+        pl.when(t < ROUNDS - 1)(lambda: g_kv.round(t))
         g_o.round(planned(t + STEPS))
         d = t - USE_AT
 
@@ -369,6 +371,8 @@
         def _():
             lax.fori_loop(2 * d - 1, 2 * d + 1, forward, 0)
             lax.fori_loop(2 * d - 1, 2 * d + 1, use, 0)
+
+        pl.when(t == ROUNDS - 1)(lambda: g_kv.others(ROWS - 1))
         return 0
 
     lax.fori_loop(0, STEPS, look, 0)

time: 108 us -> 107 us (level)
  Pallas kernels: 107 us -> 105 us
    pallas_call x1, Pallas kernels: 107 us -> 105 us  [whole(): pl.pallas_call(block_kernel, out_shape=jax.ShapeDtypeStruct((share, width...]
where the time goes in v5:
time: 107 us
  Pallas kernels  105 us (98%)
  local copies, waits for them, and re-layouts  1.57 us (1%)
    pallas_call x1, Pallas kernels, whole(): pl.pallas_call(block_kernel, out_shape=jax.ShapeDtypeStruct((share, width...  105 us

profile of v5, /device:TPU:1, one launch (start us, length us, event | category | flops | bytes accessed | tf_op | source)
XLA Modules:
  0.0 106.9 jit_solution(12137940861218406634)
XLA Ops:
  0.0 105.3 %block.1 = bf16[16,4096]{1,0:T(8,128)(2,1)} custom-call(bf16[128,4096]{1,0:T(8,128)(2,1)} %x_ref.1, bf16[64,512]{1,0:T(8,128)(2,1)} %wq_ref.1, bf16[64,128]{1,0:T(8,128)(2,1)} %wk_ref.1, bf16[64,128]{1,0:T(8,128)(2,1)} %wv_ref.1, bf16[64,512]{1,0:T(8,128)(2,1)} %bitcast.3, s32[1,128]{1,0:T(1,128)} %bitcast.5, f32[1,128]{1,0:T(1,128)} %constant.2.clone.freq_ref, ...), custom_call_target="tpu_custom_call" | custom-call | tf_op jit(solution)/shard_map/block/pallas_call | solution.py:494
  105.3 1.6 %copy.10 = bf16[16,4096]{1,0:T(8,128)(2,1)} copy(bf16[16,4096]{1,0:T(8,128)(2,1)} %block.1) | data formatting | bytes 262144

commit v6 on v5

--- a/solution.py
+++ b/solution.py
@@ -16,7 +16,7 @@
 STEPS = ROUNDS + USE_AT - 1
 O_BEGIN = 0
 O_PLAN = ((4, 1), (12, 2), (13, 3), (14, 4), (16, 5))
-MERGE_AT = 3
+MERGE_AT = 4
 NEGATIVE = -1e30
 SCALE = 1.4426950408889634 / HD ** 0.5
 

time: 107 us -> 107 us (level)
  no operation moved by 1% of the time
where the time goes in v6:
time: 107 us
  Pallas kernels  105 us (98%)
  local copies, waits for them, and re-layouts  1.57 us (1%)
    pallas_call x1, Pallas kernels, whole(): pl.pallas_call(block_kernel, out_shape=jax.ShapeDtypeStruct((share, width...  105 us

profile of v6, /device:TPU:1, one launch (start us, length us, event | category | flops | bytes accessed | tf_op | source)
XLA Modules:
  0.0 106.6 jit_solution(11077846497139868238)
XLA Ops:
  0.0 105.0 %block.1 = bf16[16,4096]{1,0:T(8,128)(2,1)} custom-call(bf16[128,4096]{1,0:T(8,128)(2,1)} %x_ref.1, bf16[64,512]{1,0:T(8,128)(2,1)} %wq_ref.1, bf16[64,128]{1,0:T(8,128)(2,1)} %wk_ref.1, bf16[64,128]{1,0:T(8,128)(2,1)} %wv_ref.1, bf16[64,512]{1,0:T(8,128)(2,1)} %bitcast.3, s32[1,128]{1,0:T(1,128)} %bitcast.5, f32[1,128]{1,0:T(1,128)} %constant.2.clone.freq_ref, ...), custom_call_target="tpu_custom_call" | custom-call | tf_op jit(solution)/shard_map/block/pallas_call | solution.py:494
  105.0 1.6 %copy.10 = bf16[16,4096]{1,0:T(8,128)(2,1)} copy(bf16[16,4096]{1,0:T(8,128)(2,1)} %block.1) | data formatting | bytes 262144
